TPU v7x, 32 devices: a whole 2x2x4 slice. The times are simulated.
32 devices in a mesh: dp: 4 (over x, core), expert: 2 (over y), tensor: 4 (over z).
Axes of the slice: x: 2, y: 2, z: 4, core: 2. Of those that a mesh axis runs over, the one named last changes fastest.
Arguments:
- block_input: bfloat16 [4096, 1024], P(('dp', 'expert')), may hold values from -6 to 6
- first_gain: float32 [1024], replicated, may hold values from 0.5 to 1.5
- w_query: bfloat16 [1024, 1024], P(None, 'tensor'), may hold values from -0.1875 to 0.1875
- key_weight: bfloat16 [1024, 512], P(None, 'tensor'), may hold values from -0.1875 to 0.1875
- value_weight: bfloat16 [1024, 512], P(None, 'tensor'), may hold values from -0.1875 to 0.1875
- w_output: bfloat16 [1024, 1024], P('tensor'), may hold values from -1 to 1
- second_gain: float32 [1024], replicated, may hold values from 0.5 to 1.5
- w_router: bfloat16 [1024, 32], replicated, may hold values from -0.09375 to 0.09375
- w_gate: bfloat16 [32, 1024, 512], P('expert', None, 'tensor'), may hold values from -0.1875 to 0.1875
- w_up: bfloat16 [32, 1024, 512], P('expert', None, 'tensor'), may hold values from -0.1875 to 0.1875
- w_down: bfloat16 [32, 512, 1024], P('expert', 'tensor'), may hold values from -1 to 1
- expert_ids: int32 [4096, 8], P(('dp', 'expert')), may hold values from 0 to 31, as said below
- slot_index: int32 [4096, 8], P(('dp', 'expert')), may hold values from -1 to 127, as said below
- piece_start_offsets: int32 [4, 2], P('dp'), may hold values from 0 to 256
- upstream: bfloat16 [4096, 1024], P(('dp', 'expert')), may hold values from -6 to 6
Outputs:
- block_output: bfloat16 [4096, 1024], P(('dp', 'expert'), 'tensor')
- grad_input: bfloat16 [4096, 1024], P(('dp', 'expert'))
- grad_first: float32 [1024], replicated
- grad_query: float32 [1024, 1024], P(None, 'tensor')
- grad_key: float32 [1024, 512], P(None, 'tensor')
- grad_value: float32 [1024, 512], P(None, 'tensor')
- grad_output: float32 [1024, 1024], P('tensor')
- grad_second: float32 [1024], replicated
- grad_router: float32 [1024, 32], replicated
- grad_gate: float32 [32, 1024, 512], P('expert', None, 'tensor')
- grad_up: float32 [32, 1024, 512], P('expert', None, 'tensor')
- grad_down: float32 [32, 512, 1024], P('expert', 'tensor')
Inputs may be any that keep to these rules, and one draw needn't show every extreme that they name: `expert_ids`: each row names 8 different experts. `slot_index`: among the rows of one device, a pair (row, k) routed to expert e holds the number of earlier pairs of that device routed to e, rows in order and k in order within a row; a pair with 128 or more earlier ones holds -1. On every device some expert receives 128 pairs or more.
All inputs are finite; a program needn't handle non-finite values.
Results may differ from a plain program's by a relative error of at most 0.02.
Values may be sent and summed in bfloat16 or wider, within the bound.
A program may use at most 192 MiB of HBM per device.

v0:
```python
import functools
import math

import jax
import jax.numpy as jnp
from jax import lax
from jax.experimental import pallas as pl
from jax.experimental.pallas import tpu as pltpu
from jax.sharding import PartitionSpec as P

HEAD_SIZE = 64
TOPK = 8
PIC = 256


epsilon = 1e-06
rope_base = 10000.0
masked_score = -1e30


def rope_tables(positions):
    steps = jnp.arange(HEAD_SIZE // 2, dtype=jnp.float32)
    inverse = jnp.exp(steps * (-2.0 * math.log(rope_base) / HEAD_SIZE))
    angle = positions.astype(jnp.float32)[:, None] * inverse[None, :]
    return (jnp.cos(angle), jnp.sin(angle))


def apply_rotary(values, cosine_table, sine_table):
    half = values.shape[-1] // 2
    first = values[..., :half]
    second = values[..., half:]
    cosine_table = cosine_table[:, None, :]
    sine_table = sine_table[:, None, :]
    return jnp.concatenate(
        [first * cosine_table - second * sine_table, second * cosine_table + first * sine_table],
        axis=-1,
    )


def unrotate(values, cosine_table, sine_table):
    half = values.shape[-1] // 2
    first = values[..., :half]
    second = values[..., half:]
    cosine_table = cosine_table[:, None, :]
    sine_table = sine_table[:, None, :]
    return jnp.concatenate(
        [first * cosine_table + second * sine_table, second * cosine_table - first * sine_table],
        axis=-1,
    )


def piece_ids(positions, offsets):
    span = 2 * PIC
    window = positions // span
    within = positions - window * span
    count = offsets.shape[0]
    match = window[:, None] == jnp.arange(count, dtype=jnp.int32)[None, :]
    start = jnp.sum(jnp.where(match, offsets[None, :], 0), axis=1)
    inside = (window < count) & (within >= start) & (within < start + PIC)
    return jnp.where(inside, window, -1)


def matmul(left, right):
    return jnp.dot(left, right, preferred_element_type=jnp.float32)


def matmul_nt(left, right):
    return lax.dot_general(
        left, right, (((1,), (1,)), ((), ())), preferred_element_type=jnp.float32
    )


def matmul_tn(left, right):
    return lax.dot_general(
        left, right, (((0,), (0,)), ((), ())), preferred_element_type=jnp.float32
    )


def norm_scale(values):
    return lax.rsqrt(jnp.mean(values * values, axis=-1, keepdims=True) + epsilon)


def norm_back(grad, unit, scale, gain):
    weighted = grad * gain
    return scale * (weighted - unit * jnp.mean(weighted * unit, axis=-1, keepdims=True))


def general_device(
    block_input,
    first_gain,
    w_query,
    key_weight,
    value_weight,
    w_output,
    second_gain,
    w_router,
    w_gate,
    w_up,
    w_down,
    expert_ids,
    slot_index,
    piece_start_offsets,
    upstream,
):
    rows_here = block_input.shape[0]
    width = block_input.shape[1]
    groups = lax.axis_size("expert")
    length = rows_here * groups
    local_heads = w_query.shape[1] // HEAD_SIZE
    local_kv = key_weight.shape[1] // HEAD_SIZE
    sharing = local_heads // local_kv
    head_rows = sharing * rows_here
    experts_all = w_router.shape[1]
    capacity = TOPK * rows_here // experts_all
    slots_all = experts_all * capacity
    score_scale = HEAD_SIZE ** (-0.5)
    positions = lax.axis_index("expert") * rows_here + jnp.arange(rows_here, dtype=jnp.int32)
    cosine_table, sine_table = rope_tables(positions)
    inputs = block_input.astype(jnp.float32)
    first_scale = norm_scale(inputs)
    first_unit = inputs * first_scale
    first_normed = (first_unit * first_gain).astype(jnp.bfloat16)
    query_rot = apply_rotary(
        matmul(first_normed, w_query).reshape(rows_here, local_heads, HEAD_SIZE),
        cosine_table,
        sine_table,
    ).astype(jnp.bfloat16)
    key_rot = (
        apply_rotary(
            matmul(first_normed, key_weight).reshape(rows_here, local_kv, HEAD_SIZE),
            cosine_table,
            sine_table,
        )
        .astype(jnp.bfloat16)
        .reshape(rows_here, local_kv * HEAD_SIZE)
    )
    value_low = matmul(first_normed, value_weight).astype(jnp.bfloat16)
    keys_all, values_all = (
        lax.all_gather(key_rot, "expert", axis=0, tiled=True),
        lax.all_gather(value_low, "expert", axis=0, tiled=True),
    )
    block = min(512, length)
    blocks = length // block

    def by_block(array):
        return array.reshape(blocks, block, local_kv, HEAD_SIZE).transpose(0, 2, 1, 3)

    def by_rows(stacked):
        return stacked.transpose(0, 2, 1, 3).reshape(length, local_kv * HEAD_SIZE)

    def head_major(array):
        return (
            array.reshape(rows_here, local_kv, sharing, HEAD_SIZE)
            .transpose(1, 2, 0, 3)
            .reshape(local_kv, head_rows, HEAD_SIZE)
        )

    def row_major(array):
        return (
            array.reshape(local_kv, sharing, rows_here, HEAD_SIZE)
            .transpose(2, 0, 1, 3)
            .reshape(rows_here, local_heads * HEAD_SIZE)
        )

    key_blocks = by_block(keys_all)
    value_blocks = by_block(values_all)
    block_starts = jnp.arange(blocks, dtype=jnp.int32) * block
    query_heads = head_major(query_rot.reshape(rows_here, local_heads * HEAD_SIZE))
    offsets = piece_start_offsets[0]
    key_pieces = piece_ids(jnp.arange(length, dtype=jnp.int32), offsets)
    query_pieces = jnp.tile(piece_ids(positions, offsets), sharing)
    query_places = jnp.tile(positions, sharing)

    def block_scores(key_block, start):
        places = start + jnp.arange(block, dtype=jnp.int32)
        pieces = lax.dynamic_slice_in_dim(key_pieces, start, block)
        causal = places[None, :] <= query_places[:, None]
        same = (pieces[None, :] == query_pieces[:, None]) & (query_pieces[:, None] >= 0)
        scores = (
            jnp.einsum("hqd,hkd->hqk", query_heads, key_block, preferred_element_type=jnp.float32)
            * score_scale
        )
        return (scores, (causal | same)[None])

    def max_step(carry, operands):
        running_max, running_sum = carry
        key_block, start = operands
        scores, allowed = block_scores(key_block, start)
        scores = jnp.where(allowed, scores, masked_score)
        new_max = jnp.maximum(running_max, jnp.max(scores, axis=-1))
        weights = jnp.where(allowed, jnp.exp(scores - new_max[..., None]), 0.0)
        new_sum = running_sum * jnp.exp(running_max - new_max) + jnp.sum(weights, axis=-1)
        return ((new_max, new_sum), None)

    start_max = jnp.full((local_kv, head_rows), masked_score, jnp.float32)
    start_sum = jnp.zeros((local_kv, head_rows), jnp.float32)
    (row_max, row_sum), _ = lax.scan(max_step, (start_max, start_sum), (key_blocks, block_starts))
    log_total = row_max + jnp.log(row_sum)

    def block_probs(key_block, start):
        scores, allowed = block_scores(key_block, start)
        return jnp.where(allowed, jnp.exp(scores - log_total[..., None]), 0.0)

    def value_step(total, operands):
        key_block, value_block, start = operands
        probs = block_probs(key_block, start).astype(jnp.bfloat16)
        return (
            total
            + jnp.einsum("hqk,hkd->hqd", probs, value_block, preferred_element_type=jnp.float32),
            None,
        )

    mixed_output, _ = lax.scan(
        value_step,
        jnp.zeros((local_kv, head_rows, HEAD_SIZE), jnp.float32),
        (key_blocks, value_blocks, block_starts),
    )
    attended = row_major(mixed_output).astype(jnp.bfloat16)
    attention = lax.psum(matmul(attended, w_output), "tensor")
    residual = inputs + attention
    second_scale = norm_scale(residual)
    second_unit = residual * second_scale
    second_normed = (second_unit * second_gain).astype(jnp.bfloat16)
    logits = matmul(second_normed, w_router)
    chosen = jnp.take_along_axis(logits, expert_ids, axis=1)
    gates = jax.nn.softmax(chosen, axis=-1)
    row_ids = jnp.arange(rows_here, dtype=jnp.int32)
    flat = jnp.where(slot_index >= 0, expert_ids * capacity + slot_index, slots_all)
    selector = (
        jnp.zeros((slots_all, rows_here), jnp.bfloat16)
        .at[flat.reshape(-1), jnp.repeat(row_ids, TOPK)]
        .set(1.0, mode="drop")
    )
    dispatched = (
        matmul(selector, second_normed).astype(jnp.bfloat16).reshape(experts_all, capacity, width)
    )
    expert_rows = lax.all_to_all(dispatched, "expert", split_axis=0, concat_axis=1, tiled=True)
    gate_in = jnp.einsum("ebd,edf->ebf", expert_rows, w_gate, preferred_element_type=jnp.float32)
    up_in = jnp.einsum("ebd,edf->ebf", expert_rows, w_up, preferred_element_type=jnp.float32)
    sigmoid_gate = jax.nn.sigmoid(gate_in)
    silu_gate = gate_in * sigmoid_gate
    hidden = (silu_gate * up_in).astype(jnp.bfloat16)
    partial_out = jnp.einsum("ebf,efd->ebd", hidden, w_down, preferred_element_type=jnp.float32)
    expert_part = lax.psum_scatter(
        partial_out.astype(jnp.bfloat16), "tensor", scatter_dimension=2, tiled=True
    )
    returned = lax.all_to_all(expert_part, "expert", split_axis=1, concat_axis=0, tiled=True)
    quarter = returned.shape[2]
    padded_out = jnp.concatenate(
        [returned.reshape(slots_all, quarter), jnp.zeros((1, quarter), jnp.bfloat16)], axis=0
    )
    feature_start = lax.axis_index("tensor") * quarter
    grad_full = upstream.astype(jnp.float32)
    grad_part = lax.dynamic_slice_in_dim(grad_full, feature_start, quarter, 1)
    mixture = jnp.zeros((rows_here, quarter), jnp.float32)
    gate_terms = []
    for pick in range(TOPK):
        picked = padded_out[flat[:, pick]].astype(jnp.float32)
        mixture = mixture + gates[:, pick : pick + 1] * picked
        gate_terms.append(jnp.sum(grad_part * picked, axis=1))
    gate_part = jnp.stack(gate_terms, axis=1)
    block_output = (lax.dynamic_slice_in_dim(residual, feature_start, quarter, 1) + mixture).astype(
        jnp.bfloat16
    )
    slot_gates = (
        jnp.zeros((slots_all + 1,), jnp.float32)
        .at[flat.reshape(-1)]
        .set(gates.reshape(-1))[:slots_all]
    )
    grad_slots = (
        (matmul(selector, upstream) * slot_gates[:, None])
        .astype(jnp.bfloat16)
        .reshape(experts_all, capacity, width)
    )
    grad_rows_in = lax.all_to_all(grad_slots, "expert", split_axis=0, concat_axis=1, tiled=True)
    hidden_grad = jnp.einsum(
        "ebd,efd->ebf", grad_rows_in, w_down, preferred_element_type=jnp.float32
    )
    grad_down = jnp.einsum("ebf,ebd->efd", hidden, grad_rows_in, preferred_element_type=jnp.float32)
    gate_in_grad = (
        hidden_grad * up_in * (sigmoid_gate * (1.0 + gate_in * (1.0 - sigmoid_gate)))
    ).astype(jnp.bfloat16)
    up_in_grad = (hidden_grad * silu_gate).astype(jnp.bfloat16)
    grad_gate = jnp.einsum(
        "ebd,ebf->edf", expert_rows, gate_in_grad, preferred_element_type=jnp.float32
    )
    grad_up = jnp.einsum(
        "ebd,ebf->edf", expert_rows, up_in_grad, preferred_element_type=jnp.float32
    )
    rows_part = jnp.einsum("ebf,edf->ebd", gate_in_grad, w_gate, preferred_element_type=jnp.float32)
    rows_part = rows_part + jnp.einsum(
        "ebf,edf->ebd", up_in_grad, w_up, preferred_element_type=jnp.float32
    )
    rows_back = lax.all_to_all(
        rows_part.astype(jnp.bfloat16), "expert", split_axis=1, concat_axis=0, tiled=True
    ).astype(rows_part.dtype)
    padded_back = jnp.concatenate(
        [rows_back.reshape(slots_all, width), jnp.zeros((1, width), jnp.float32)], axis=0
    )
    second_part = jnp.zeros((rows_here, width), jnp.float32)
    for pick in range(TOPK):
        second_part = second_part + padded_back[flat[:, pick]]
    second_sum, gate_grads = (
        lax.psum(second_part.astype(jnp.bfloat16), "tensor").astype(jnp.float32),
        lax.psum(gate_part.astype(jnp.bfloat16), "tensor").astype(jnp.float32),
    )
    chosen_grad = gates * (gate_grads - jnp.sum(gates * gate_grads, axis=1, keepdims=True))
    expert_axis = jnp.arange(experts_all, dtype=jnp.int32)
    logit_grad = jnp.zeros((rows_here, experts_all), jnp.float32)
    for pick in range(TOPK):
        logit_grad = logit_grad + jnp.where(
            expert_ids[:, pick : pick + 1] == expert_axis[None, :],
            chosen_grad[:, pick : pick + 1],
            0.0,
        )
    logit_low = logit_grad.astype(jnp.bfloat16)
    grad_router = matmul_tn(second_normed, logit_low)
    second_grad = second_sum + matmul_nt(logit_low, w_router)
    grad_second = jnp.sum(second_grad * second_unit, axis=0)
    residual_grad = grad_full + norm_back(second_grad, second_unit, second_scale, second_gain)
    residual_low = residual_grad.astype(jnp.bfloat16)
    grad_output = matmul_tn(attended, residual_low)
    attended_grad = head_major(matmul_nt(residual_low, w_output).astype(jnp.bfloat16))

    def delta_step(total, operands):
        key_block, value_block, start = operands
        probs = block_probs(key_block, start)
        prob_grad = jnp.einsum(
            "hqd,hkd->hqk", attended_grad, value_block, preferred_element_type=jnp.float32
        )
        return (total + jnp.sum(probs * prob_grad, axis=-1), None)

    delta, _ = lax.scan(
        delta_step,
        jnp.zeros((local_kv, head_rows), jnp.float32),
        (key_blocks, value_blocks, block_starts),
    )

    def grad_step(query_total, operands):
        key_block, value_block, start = operands
        probs = block_probs(key_block, start)
        prob_grad = jnp.einsum(
            "hqd,hkd->hqk", attended_grad, value_block, preferred_element_type=jnp.float32
        )
        score_grad = (probs * (prob_grad - delta[..., None])).astype(jnp.bfloat16)
        query_total = (
            query_total
            + jnp.einsum("hqk,hkd->hqd", score_grad, key_block, preferred_element_type=jnp.float32)
            * score_scale
        )
        key_grad = (
            jnp.einsum("hqk,hqd->hkd", score_grad, query_heads, preferred_element_type=jnp.float32)
            * score_scale
        )
        value_grad = jnp.einsum(
            "hqk,hqd->hkd",
            probs.astype(jnp.bfloat16),
            attended_grad,
            preferred_element_type=jnp.float32,
        )
        return (query_total, (key_grad, value_grad))

    query_total, (key_stack, value_stack) = lax.scan(
        grad_step,
        jnp.zeros((local_kv, head_rows, HEAD_SIZE), jnp.float32),
        (key_blocks, value_blocks, block_starts),
    )
    key_back, value_back = (
        lax.psum_scatter(
            by_rows(key_stack).astype(jnp.bfloat16), "expert", scatter_dimension=0, tiled=True
        ).astype(jnp.float32),
        lax.psum_scatter(
            by_rows(value_stack).astype(jnp.bfloat16), "expert", scatter_dimension=0, tiled=True
        ).astype(jnp.float32),
    )
    query_grad = (
        unrotate(
            row_major(query_total).reshape(rows_here, local_heads, HEAD_SIZE),
            cosine_table,
            sine_table,
        )
        .astype(jnp.bfloat16)
        .reshape(rows_here, local_heads * HEAD_SIZE)
    )
    key_grad = (
        unrotate(key_back.reshape(rows_here, local_kv, HEAD_SIZE), cosine_table, sine_table)
        .astype(jnp.bfloat16)
        .reshape(rows_here, local_kv * HEAD_SIZE)
    )
    value_grad = value_back.astype(jnp.bfloat16)
    grad_query = matmul_tn(first_normed, query_grad)
    grad_key = matmul_tn(first_normed, key_grad)
    grad_value = matmul_tn(first_normed, value_grad)
    first_part = (
        matmul_nt(query_grad, w_query)
        + matmul_nt(key_grad, key_weight)
        + matmul_nt(value_grad, value_weight)
    )
    first_grad = lax.psum(first_part.astype(jnp.bfloat16), "tensor").astype(jnp.float32)
    grad_first = jnp.sum(first_grad * first_unit, axis=0)
    grad_input = (
        residual_grad + norm_back(first_grad, first_unit, first_scale, first_gain)
    ).astype(jnp.bfloat16)
    dense = lax.psum(
        (grad_query, grad_key, grad_value, grad_output, grad_router, grad_first, grad_second),
        ("dp", "expert"),
    )
    expert_sums = (
        lax.psum(grad_gate.astype(jnp.bfloat16), "dp").astype(jnp.float32),
        lax.psum(grad_up.astype(jnp.bfloat16), "dp").astype(jnp.float32),
        lax.psum(grad_down.astype(jnp.bfloat16), "dp").astype(jnp.float32),
    )
    return (
        block_output,
        grad_input,
        dense[5],
        dense[0],
        dense[1],
        dense[2],
        dense[3],
        dense[6],
        dense[4],
        expert_sums[0],
        expert_sums[1],
        expert_sums[2],
    )


BF = jnp.bfloat16
F32 = jnp.float32
MIB = 1 << 20


def vmem_spec():
    return pl.BlockSpec(memory_space=pltpu.VMEM)


def smem_spec():
    return pl.BlockSpec(memory_space=pltpu.SMEM)


def allowed_pairs(offsets_ref, rows, start, count):
    side = lax.axis_index("expert")
    here = start + lax.broadcasted_iota(jnp.int32, (count, 1), 0)
    keys = lax.broadcasted_iota(jnp.int32, (1, 2 * rows), 1)
    query_place = side * rows + here
    key_place = jnp.where(keys < rows, side * rows + keys, (1 - side) * rows + keys - rows)
    span = 2 * PIC

    def piece(places):
        window = places // span
        within = places - window * span
        start = jnp.where(window == 0, offsets_ref[0, 0], offsets_ref[0, 1])
        inside = (within >= start) & (within < start + PIC)
        return jnp.where(inside, window, -1)

    query_piece = piece(query_place)
    key_piece = piece(key_place)
    return (key_place <= query_place) | ((key_piece == query_piece) & (query_piece >= 0))


def turn(values, first):
    wide = values.shape[1]
    half = HEAD_SIZE // 2
    return jnp.where(
        first, -pltpu.roll(values, wide - half, 1), pltpu.roll(values, half, 1)
    )


MESH = pl.DeviceIdType.MESH
PART = 32
LAG = 3
LINK_COST = pl.CostEstimate(flops=4 * 10**10, bytes_accessed=10**7, transcendentals=0)


def meet(partners):
    barrier = pltpu.get_barrier_semaphore()
    count = 0
    for here, device in partners:
        here = jnp.asarray(here)

        @pl.when(here)
        def _():
            pl.semaphore_signal(barrier, inc=1, device_id=device, device_id_type=MESH)

        count = count + here.astype(jnp.int32)
    pl.semaphore_wait(barrier, count)


def line_partners():
    place = lax.axis_index("tensor")
    last = lax.axis_size("tensor") - 1
    return [(place > 0, {"tensor": place - 1}), (place < last, {"tensor": place + 1})]


class Line:
    def __init__(self, parts, term, from_left, from_right, to_right, to_left, sems):
        self.place = lax.axis_index("tensor")
        self.last = lax.axis_size("tensor") - 1
        self.parts = parts
        self.term = term
        self.from_left, self.from_right = from_left, from_right
        self.to_right, self.to_left = to_right, to_left
        self.sems = sems

    def copy(self, way, at):
        near = jnp.where(self.place < self.last, self.place + 1, self.place - 1)
        far = jnp.where(self.place > 0, self.place - 1, self.place + 1)
        source, target, device = (
            (self.to_right, self.from_left, near) if way == 0 else (self.to_left, self.from_right, far)
        )
        return pltpu.make_async_remote_copy(
            src_ref=source.at[at],
            dst_ref=target.at[at],
            send_sem=self.sems.at[2 * way, at],
            recv_sem=self.sems.at[2 * way + 1, at],
            device_id={"tensor": device},
            device_id_type=MESH,
        )

    def clear(self):
        @pl.when(self.place == 0)
        def _():
            self.from_left[...] = jnp.zeros(self.from_left.shape, self.from_left.dtype)

        @pl.when(self.place == self.last)
        def _():
            self.from_right[...] = jnp.zeros(self.from_right.shape, self.from_right.dtype)

    def step(self, at):
        for way in range(2):
            part = at - LAG * (self.place if way == 0 else self.last - self.place)
            has_source = self.place > 0 if way == 0 else self.place < self.last
            has_target = self.place < self.last if way == 0 else self.place > 0
            arrived = self.from_left if way == 0 else self.from_right
            leaving = self.to_right if way == 0 else self.to_left
            valid = (part >= 0) & (part < self.parts)

            @pl.when(valid & has_source)
            def _():
                self.copy(way, part).wait_recv()

            @pl.when(valid & has_target)
            def _():
                leaving[part] = (self.term(part) + arrived[part].astype(F32)).astype(BF)
                self.copy(way, part).start()

    def total(self, part):
        return self.term(part) + self.from_left[part].astype(F32) + self.from_right[part].astype(F32)

    def drain(self):
        def wait(part, carry):
            @pl.when(self.place < self.last)
            def _():
                self.copy(0, part).wait_send()

            @pl.when(self.place > 0)
            def _():
                self.copy(1, part).wait_send()

            return carry

        lax.fori_loop(0, self.parts, wait, 0)


def line_scratch(parts, width):
    return [pltpu.VMEM((parts, PART, width), BF)] * 4 + [pltpu.SemaphoreType.DMA((4, parts))]


def peer_copy(source, target, sems, at):
    return pltpu.make_async_remote_copy(
        src_ref=source,
        dst_ref=target,
        send_sem=sems.at[0, at],
        recv_sem=sems.at[1, at],
        device_id={"expert": 1 - lax.axis_index("expert")},
        device_id_type=MESH,
    )


def scale_of(values):
    return lax.rsqrt(jnp.mean(values * values, axis=-1, keepdims=True) + epsilon)


def plain_copy(source, target, sems, at, device):
    return pltpu.make_async_remote_copy(
        src_ref=source, dst_ref=target, send_sem=sems.at[0, at], recv_sem=sems.at[1, at],
        device_id=device, device_id_type=MESH,
    )


def beside():
    return {"dp": lax.rem(lax.axis_index("dp") + 2, 4)}


def other_core():
    place = lax.axis_index("dp")
    return {"dp": place + 1 - 2 * lax.rem(place, 2)}


EARLY = 64
BAND = 256


def front_kernel(
    offsets_ref, x_ref, gain1_ref, gain2_ref, wq_ref, wk_ref, wv_ref, wo_ref, cos_ref, sin_ref, ids_ref, slots_ref, up_hbm,
    n1_ref, q_ref, k_ref, v_ref, att_ref, lse_ref, res_ref, n_ref, marks_ref, far_marks, up_peer, far_up,
    from_left, from_right, to_right, to_left, sems, peer_sems, far_sems, terms,
):
    parts = x_ref.shape[0]
    rows, width = n1_ref.shape
    side = lax.axis_index("expert")
    peer = {"expert": 1 - side}
    line = Line(parts, lambda at: terms[at], from_left, from_right, to_right, to_left, sems)
    meet(line_partners() + [(True, peer), (True, beside())])
    early, late = pl.ds(0, EARLY), pl.ds(EARLY, rows - EARLY)
    up_early = plain_copy(up_hbm.at[early, :], up_peer.at[early, :], far_sems, 0, peer)
    up_late = plain_copy(up_hbm.at[late, :], up_peer.at[late, :], far_sems, 1, peer)
    up_cross = plain_copy(up_hbm, far_up, far_sems, 2, beside())
    key_copy = plain_copy(k_ref.at[0], k_ref.at[1], far_sems, 3, peer)
    value_copy = plain_copy(v_ref.at[0], v_ref.at[1], far_sems, 4, peer)
    marks_copy = plain_copy(marks_ref.at[0], marks_ref.at[1], far_sems, 5, peer)
    marks_cross = plain_copy(marks_ref, far_marks, far_sems, 6, beside())
    up_early.start()
    up_cross.start()
    line.clear()

    values = x_ref[...].reshape(rows, width).astype(F32)
    normed = (values * scale_of(values) * gain1_ref[...]).astype(BF)
    n1_ref[...] = normed
    queries, kv = q_ref.shape[1], k_ref.shape[2]

    def rotate(array):
        wide = array.shape[1]
        lane = lax.broadcasted_iota(jnp.int32, (1, wide), 1)
        first = lane % HEAD_SIZE < HEAD_SIZE // 2
        cosines = jnp.concatenate([cos_ref[...]] * (wide // 128), axis=1)
        sines = jnp.concatenate([sin_ref[...]] * (wide // 128), axis=1)
        return (array * cosines + turn(array, first) * sines).astype(BF)

    k_ref[0] = rotate(matmul(normed, wk_ref[...]))
    key_copy.start()
    v_ref[0] = matmul(normed, wv_ref[...]).astype(BF)
    value_copy.start()
    experts_all = marks_ref.shape[2] // 2
    names = lax.broadcasted_iota(jnp.int32, (experts_all, 1), 0)
    chosen = jnp.zeros((experts_all, rows), F32)
    kept = jnp.zeros((experts_all, rows), F32)
    for pick in range(ids_ref.shape[0]):
        hit = jnp.where(ids_ref[pick : pick + 1, :] == names, 1.0, 0.0)
        chosen = chosen + hit
        kept = kept + jnp.where(slots_ref[pick : pick + 1, :] >= 0, hit, 0.0)
    marks_ref[0] = jnp.concatenate([chosen, kept], axis=0).T.astype(BF)
    marks_copy.start()
    up_late.start()
    q_ref[...] = rotate(matmul(normed, wq_ref[...]))
    key_copy.wait_recv()
    value_copy.wait_recv()
    sharing = queries // kv

    def attend(at):
        start = pl.multiple_of(at * BAND, BAND)
        band = pl.ds(start, BAND)
        allowed = allowed_pairs(offsets_ref, rows, start, BAND)
        pieces = []
        for head in range(queries // HEAD_SIZE):
            kv_at = head // sharing * HEAD_SIZE
            query = q_ref[band, head * HEAD_SIZE : (head + 1) * HEAD_SIZE]
            key = k_ref[:, :, kv_at : kv_at + HEAD_SIZE].reshape(2 * rows, HEAD_SIZE)
            value = v_ref[:, :, kv_at : kv_at + HEAD_SIZE].reshape(2 * rows, HEAD_SIZE)
            scores = jnp.where(allowed, matmul_nt(query, key) * (HEAD_SIZE**-0.5), masked_score)
            peak = jnp.max(scores, axis=1, keepdims=True)
            weights = jnp.exp(scores - peak)
            total = jnp.sum(weights, axis=1, keepdims=True)
            pieces.append(matmul((weights * (1.0 / total)).astype(BF), value))
            lse_ref[band, head : head + 1] = peak + jnp.log(total)
        attended = jnp.concatenate(pieces, axis=1).astype(BF)
        att_ref[band, :] = attended
        count = BAND // PART
        terms[pl.ds(at * count, count)] = matmul(attended, wo_ref[...]).reshape(count, PART, width)

    def body(at, carry):
        @pl.when(at < rows // BAND)
        def _():
            attend(at)

        @pl.when(at == 3)
        def _():
            marks_copy.wait_recv()
            marks_cross.start()

        line.step(at - 1)
        part = at - 1 - LAG * line.last

        @pl.when(part >= 0)
        def _():
            residual = x_ref[part].astype(F32) + line.total(part)
            res_ref[part] = residual
            unit = residual * scale_of(residual)
            n_ref[0, part] = (unit * gain2_ref[...]).astype(BF)
            peer_copy(n_ref.at[0, part], n_ref.at[1, part], peer_sems, part).start()

        return carry

    lax.fori_loop(0, 1 + parts + LAG * line.last, body, 0)
    line.drain()
    for copy in (key_copy, value_copy, marks_copy):
        copy.wait_send()
    for copy in (up_early, up_late, up_cross, marks_cross):
        copy.wait()

    def wait(part, carry):
        peer_copy(n_ref.at[0, part], n_ref.at[1, part], peer_sems, part).wait()
        return carry

    lax.fori_loop(0, parts, wait, 0)


def front(
    offsets, block_input, first_gain, second_gain, w_query, key_weight, value_weight, w_output, cosines, sines,
    expert_ids, slot_index, upstream, experts_all,
):
    rows, width = block_input.shape
    parts = rows // PART
    queries, kv = w_query.shape[1], key_weight.shape[1]
    any_spec = pl.BlockSpec(memory_space=pl.ANY)
    low = lambda *shape: jax.ShapeDtypeStruct(shape, BF)
    return pl.pallas_call(
        front_kernel,
        out_shape=(
            low(rows, width),
            low(rows, queries),
            low(2, rows, kv),
            low(2, rows, kv),
            low(rows, queries),
            jax.ShapeDtypeStruct((rows, 128), F32),
            jax.ShapeDtypeStruct((parts, PART, width), F32),
            low(2, parts, PART, width),
            low(2, rows, 2 * experts_all),
            low(2, rows, 2 * experts_all),
            low(rows, width),
            low(rows, width),
        ),
        in_specs=[smem_spec()] + [vmem_spec()] * 11 + [any_spec],
        out_specs=(vmem_spec(),) * 9 + (any_spec,) * 3,
        scratch_shapes=line_scratch(parts, width)
        + [
            pltpu.SemaphoreType.DMA((2, parts)),
            pltpu.SemaphoreType.DMA((2, 7)),
            pltpu.VMEM((parts, PART, width), F32),
        ],
        compiler_params=pltpu.CompilerParams(
            collective_id=0, has_side_effects=True, vmem_limit_bytes=60 * MIB
        ),
        cost_estimate=LINK_COST,
        name="front",
    )(
        offsets, block_input.reshape(parts, PART, width), first_gain[None], second_gain[None], w_query, key_weight,
        value_weight, w_output, cosines, sines, expert_ids, slot_index, upstream,
    )


UNIT = 512
SUB = 256


def residual_grad_kernel(
    back_ref, route_ref, res_ref, up_ref, gain_ref, wr_ref, mix_ref,
    far_n, far_on, far_g0, far_g1, far_og0, far_og1, far_m, far_om,
    wg_hbm, wu_hbm, wd_hbm, pg_hbm, pu_hbm, pd_hbm,
    grad_ref, low_ref, second_ref, route_out, mixed_ref, sg_hbm, su_hbm, sd_hbm, og_hbm, ou_hbm, od_hbm,
    from_left, from_right, to_right, to_left, sems, peer_sems, arrived, terms,
    tokens_n, tokens_g, turned, kept_gates, gates_w, ups_w, downs_w, pair_g, pair_u, pair_d, ght, dgs, dus,
    row_sems, weight_sems, pair_sems, out_sems, mix_arrived, mix_sems, marks_ref, share_sems,
):
    parts = back_ref.shape[1]
    core = lax.rem(lax.axis_index("dp"), 2)
    side = lax.axis_index("expert")
    groups, group, width, hid = pair_g.shape
    experts_all = wr_ref.shape[0]
    line = Line(parts + 1, lambda at: terms[at], from_left, from_right, to_right, to_left, sems)
    line.clear()
    meet(line_partners() + [(True, {"expert": 1 - side}), (True, other_core())])

    def send(part, carry):
        peer_copy(back_ref.at[1, part], arrived.at[part], peer_sems, part).start()
        return carry

    lax.fori_loop(0, parts, send, 0)

    def send_mix(part, carry):
        peer_copy(mix_ref.at[1, part], mix_arrived.at[part], mix_sems, part).start()
        return carry

    lax.fori_loop(0, parts, send_mix, 0)
    half = tokens_n.shape[0] // 2
    quarter = half // 2
    row_copies = []
    for place, (rows, first, second, marks) in enumerate(((far_n, far_g0, far_g1, far_m), (far_on, far_og0, far_og1, far_om))):
        at = place * half
        row_copies += [
            pltpu.make_async_copy(rows, tokens_n.at[pl.ds(at, half), :], row_sems.at[0, place]),
            pltpu.make_async_copy(first, tokens_g.at[pl.ds(at, quarter), :], row_sems.at[1, place]),
            pltpu.make_async_copy(second, tokens_g.at[pl.ds(at + quarter, quarter), :], row_sems.at[2, place]),
            pltpu.make_async_copy(marks, marks_ref.at[pl.ds(at, half), :], row_sems.at[3, place]),
        ]
    weight_copies, pair_copies, out_copies = [], [], []
    for at in range(groups):
        first = core * (groups * group) + at * group
        weight_copies.append(
            [
                pltpu.make_async_copy(
                    source.at[first + expert],
                    target.at[at, :, pl.ds(expert * hid, hid)],
                    weight_sems.at[at, kind, expert],
                )
                for expert in range(group)
                for kind, (source, target) in enumerate(((wg_hbm, gates_w), (wu_hbm, ups_w)))
            ]
            + [pltpu.make_async_copy(wd_hbm.at[pl.ds(first, group)], downs_w.at[at], weight_sems.at[at, 2, 0])]
        )
        sources = (pg_hbm, pu_hbm, pd_hbm)
        held = (pair_g, pair_u, pair_d)
        targets = (sg_hbm, su_hbm, sd_hbm)
        others = (og_hbm, ou_hbm, od_hbm)
        pair_copies.append(
            [
                pltpu.make_async_copy(sources[kind].at[pl.ds(at * group, group)], held[kind].at[at], pair_sems.at[at, kind])
                for kind in range(3)
            ]
        )
        out_copies.append(
            [
                pltpu.make_async_copy(held[kind].at[at], targets[kind].at[pl.ds(at * group, group)], out_sems.at[at, kind])
                for kind in range(3)
            ]
            + [
                plain_copy(
                    held[kind].at[at], others[kind].at[pl.ds(at * group, group)], share_sems.at[at], kind, other_core()
                )
                for kind in range(3)
            ]
        )
    for copy in row_copies[:4] + weight_copies[0] + row_copies[4:] + pair_copies[0] + weight_copies[1] + pair_copies[1]:
        copy.start()
    terms[parts] = route_ref[...]
    second_ref[...] = jnp.zeros(second_ref.shape, F32)
    chunks = 2 * half // UNIT
    units = chunks + 3

    def compute(at):
        for where in range(groups):
            unit = at - where * units

            @pl.when(unit == 0)
            def _():
                for copy in weight_copies[where]:
                    copy.wait()

            if where == 0:

                @pl.when(unit == 0)
                def _():
                    for copy in row_copies[:4]:
                        copy.wait()

                @pl.when(unit == half // UNIT)
                def _():
                    for copy in row_copies[4:]:
                        copy.wait()

            @pl.when(unit == chunks)
            def _():
                for copy in pair_copies[where]:
                    copy.wait()

        where = at // units
        unit = at - where * units

        @pl.when(unit < chunks)
        def _():
            down = downs_w[where].reshape(group * hid, width)
            column = side * (experts_all // 2) + (core * groups + where) * group
            for sub in range(UNIT // SUB):
                rows = pl.ds(pl.multiple_of(unit * UNIT + sub * SUB, SUB), SUB)

                @pl.when(where == 0)
                def _():
                    token = tokens_n[rows, :]
                    kept_gates[rows, :] = route_gates(token, marks_ref[rows, :], wr_ref[...])[1]
                    turned[:, rows] = token.T

            for sub in range(UNIT // SUB):
                rows = pl.ds(pl.multiple_of(unit * UNIT + sub * SUB, SUB), SUB)
                pulled = matmul_nt(tokens_g[rows, :], down)
                weight = spread_gates(kept_gates[rows, :], column, group, hid)
                _, gated, gate_grad, up_grad = hidden_terms(
                    tokens_n[rows, :], pulled, weight, gates_w[where], ups_w[where]
                )
                ght[:, rows] = gated.T
                dgs[rows, :] = gate_grad
                dus[rows, :] = up_grad

        @pl.when((unit >= chunks) & (unit < chunks + 2))
        def _():
            rows = pl.ds(pl.multiple_of((unit - chunks) * (width // 2), width // 2), width // 2)
            for source, held in ((dgs, pair_g), (dus, pair_u)):
                part = matmul(turned[rows, :], source[...])
                for expert in range(group):
                    more = part[:, expert * hid : (expert + 1) * hid]
                    held[where, expert, rows, :] = (held[where, expert, rows, :].astype(F32) + more).astype(BF)

        @pl.when(unit == chunks + 2)
        def _():
            part = matmul(ght[...], tokens_g[...])
            for expert in range(group):
                more = part[expert * hid : (expert + 1) * hid, :]
                pair_d[where, expert] = (pair_d[where, expert].astype(F32) + more).astype(BF)

        for where in range(groups):

            @pl.when(at == where * units + units - 1)
            def _():
                for copy in out_copies[where]:
                    copy.start()

    def add_mix(part):
        peer_copy(mix_ref.at[1, part], mix_arrived.at[part], mix_sems, part).wait_recv()
        mixed_ref[part] = (mix_ref[0, part].astype(F32) + mix_arrived[part].astype(F32)).astype(BF)

    steps = parts + 1 + LAG * line.last

    def advance(at):
        @pl.when(at < parts)
        def _():
            peer_copy(back_ref.at[1, at], arrived.at[at], peer_sems, at).wait_recv()
            terms[at] = back_ref[0, at].astype(F32) + arrived[at].astype(F32)

        line.step(at)
        part = at - LAG * line.last

        @pl.when((part >= 0) & (part < parts))
        def _():
            grad = line.total(part)
            residual = res_ref[part]
            scale = scale_of(residual)
            unit = residual * scale
            second_ref[...] += jnp.sum(grad * unit, axis=0, keepdims=True)
            result = up_ref[part].astype(F32) + norm_back(grad, unit, scale, gain_ref[...])
            grad_ref[part] = result
            low_ref[part] = result.astype(BF)

        @pl.when((at >= MIX_STEP) & (at < MIX_STEP + parts))
        def _():
            add_mix(at - MIX_STEP)

    turns = max(groups * units, (steps + 1) // 2)

    def body(at, carry):
        @pl.when(at < groups * units)
        def _():
            compute(at)

        def pair(half, carry):
            advance(2 * at + half)
            return carry

        lax.fori_loop(0, 2, pair, 0)
        return carry

    lax.fori_loop(0, turns, body, 0)
    route_out[...] = line.total(parts)

    def rest(part, carry):
        add_mix(part)
        return carry

    lax.fori_loop(2 * turns - MIX_STEP, parts, rest, 0)
    line.drain()

    def wait(part, carry):
        peer_copy(back_ref.at[1, part], arrived.at[part], peer_sems, part).wait_send()
        peer_copy(mix_ref.at[1, part], mix_arrived.at[part], mix_sems, part).wait_send()
        return carry

    lax.fori_loop(0, parts, wait, 0)
    for copies in out_copies:
        for copy in copies:
            copy.wait()


MIX_STEP = 17


def residual_gradient(back, mix, route, residual, upstream, gain, w_router, far_rows, w_gate, w_up, w_down, pairs):
    rows, width = upstream.shape
    parts = rows // PART
    half, _, hid = pairs[0].shape
    groups = half // GROUP
    tokens = 2 * far_rows[0].shape[0]
    any_spec = pl.BlockSpec(memory_space=pl.ANY)
    grad, low, second, route, mixed, *sums = pl.pallas_call(
        residual_grad_kernel,
        out_shape=[
            jax.ShapeDtypeStruct((parts, PART, width), F32),
            jax.ShapeDtypeStruct((parts, PART, width), BF),
            jax.ShapeDtypeStruct((1, width), F32),
            jax.ShapeDtypeStruct(route.shape, F32),
            jax.ShapeDtypeStruct((parts, PART, width), BF),
        ]
        + [jax.ShapeDtypeStruct(pair.shape, BF) for pair in pairs] * 2,
        in_specs=[vmem_spec()] * 7 + [any_spec] * 14,
        out_specs=[vmem_spec()] * 5 + [any_spec] * 6,
        scratch_shapes=line_scratch(parts + 1, width)
        + [
            pltpu.SemaphoreType.DMA((2, parts)),
            pltpu.VMEM((parts, PART, width), BF),
            pltpu.VMEM((parts + 1, PART, width), F32),
            pltpu.VMEM((tokens, width), BF),
            pltpu.VMEM((tokens, width), BF),
            pltpu.VMEM((width, tokens), BF),
            pltpu.VMEM((tokens, w_router.shape[0]), F32),
            pltpu.VMEM((groups, width, GROUP * hid), BF),
            pltpu.VMEM((groups, width, GROUP * hid), BF),
            pltpu.VMEM((groups, GROUP, hid, width), BF),
            pltpu.VMEM((groups, GROUP, width, hid), BF),
            pltpu.VMEM((groups, GROUP, width, hid), BF),
            pltpu.VMEM((groups, GROUP, hid, width), BF),
            pltpu.VMEM((GROUP * hid, tokens), BF),
            pltpu.VMEM((tokens, GROUP * hid), BF),
            pltpu.VMEM((tokens, GROUP * hid), BF),
            pltpu.SemaphoreType.DMA((4, 2)),
            pltpu.SemaphoreType.DMA((groups, 3, GROUP)),
            pltpu.SemaphoreType.DMA((groups, 3)),
            pltpu.SemaphoreType.DMA((groups, 3)),
            pltpu.VMEM((parts, PART, width), BF),
            pltpu.SemaphoreType.DMA((2, parts)),
            pltpu.VMEM((tokens, 2 * w_router.shape[0]), BF),
            pltpu.SemaphoreType.DMA((groups, 2, 3)),
        ],
        compiler_params=pltpu.CompilerParams(
            collective_id=1, has_side_effects=True, vmem_limit_bytes=60 * MIB
        ),
        cost_estimate=LINK_COST,
        name="residual_grad",
    )(
        back.reshape(2, parts, PART, width), route, residual, upstream.reshape(parts, PART, width), gain[None],
        w_router, mix.reshape(2, parts, PART, width), *far_rows, w_gate, w_up, w_down, *pairs,
    )
    return grad, low.reshape(rows, width), second, route, mixed, sums


def input_grad_kernel(
    offsets_ref, x_ref, res_grad_ref, gain_ref, n_ref, wq_ref, wk_ref, wv_ref, wo_ref, cos_ref, sin_ref,
    q_ref, k_ref, v_ref, lse_ref, att_ref, low_ref, route_ref, second_ref, mix_ref, res_ref,
    grad_ref, wide_out, wide_back, tall_out, tall_back, gains_ref, block_ref,
    from_left, from_right, to_right, to_left, sems, terms, kv_out, kv_in, kv_sems,
    wide, wide_core, wide_x, wide_y, tall, tall_core, tall_x, tall_y, rows2, rows_core, rows_x, rows_y, sum_sems,
    mix_left, mix_right, mix_to_right, mix_to_left, mix_sems,
):
    parts = x_ref.shape[0]
    rows = n_ref.shape[0]
    width = n_ref.shape[1]
    core = lax.rem(lax.axis_index("dp"), 2)
    peer = {"expert": 1 - lax.axis_index("expert")}
    kv = wk_ref.shape[1]
    queries = wq_ref.shape[1]
    line = Line(parts + 1, lambda at: terms[at], from_left, from_right, to_right, to_left, sems)
    spread = Spread(mix_ref, mix_left, mix_right, mix_to_right, mix_to_left, mix_sems)
    line.clear()
    spread.clear()
    meet(line_partners() + [(True, peer), (True, beside()), (True, other_core())])
    spread.step(0)
    key_copy = plain_copy(kv_out.at[0, pl.ds(rows, rows), :], kv_in.at[0], kv_sems, 0, peer)
    value_copy = plain_copy(kv_out.at[1, pl.ds(rows, rows), :], kv_in.at[1], kv_sems, 1, peer)

    scale = HEAD_SIZE**-0.5
    low = low_ref[...]
    out_part = matmul(att_ref[...].T, low).astype(BF)
    att_grad = matmul_nt(low, wo_ref[...]).astype(BF)
    half_tall = tall.shape[1]
    outs = wo_ref.shape[0]
    for at in range(2):
        start, high = at * half_tall, (at + 1) * half_tall
        top = min(high, outs)
        tall[at, : top - start, :] = out_part[start:top, :]
        if high > outs:
            tall[at, outs - start :, :] = route_ref[...].astype(BF)

    tall_steps = [
        plain_copy(tall.at[1 - core], tall_core, sum_sems, 0, other_core()),
        plain_copy(tall.at[core], tall_y, sum_sems, 1, peer),
        plain_copy(tall.at[core], tall_x, sum_sems, 2, beside()),
        plain_copy(tall.at[core], tall_back, sum_sems, 3, other_core()),
    ]
    wide_steps = [
        plain_copy(wide.at[1 - core], wide_core, sum_sems, 4, other_core()),
        plain_copy(wide.at[core], wide_x, sum_sems, 5, beside()),
        plain_copy(wide.at[core], wide_y, sum_sems, 6, peer),
        plain_copy(wide.at[core], wide_back, sum_sems, 7, other_core()),
    ]
    rows_steps = [
        plain_copy(rows2, rows_core, sum_sems, 8, other_core()),
        plain_copy(rows2, rows_y, sum_sems, 9, peer),
        plain_copy(rows2, rows_x, sum_sems, 10, beside()),
    ]
    tall_steps[0].start()

    def add(held, arrived):
        held[...] = (held[...].astype(F32) + arrived[...].astype(F32)).astype(BF)

    allowed = allowed_pairs(offsets_ref, rows, 0, rows)
    sharing = queries // kv
    query_parts, key_parts, value_parts = [], [], []
    for head in range(queries // HEAD_SIZE):
        if head:
            spread.step(head)
        if head == 1:
            tall_steps[0].wait()
            add(tall.at[core], tall_core)
            tall_steps[1].start()
        if head == 3:
            tall_steps[1].wait()
            add(tall.at[core], tall_y)
            tall_steps[2].start()
        at = head * HEAD_SIZE
        kv_at = head // sharing * HEAD_SIZE
        query = q_ref[:, at : at + HEAD_SIZE]
        key = k_ref[:, kv_at : kv_at + HEAD_SIZE]
        value = v_ref[:, kv_at : kv_at + HEAD_SIZE]
        grad = att_grad[:, at : at + HEAD_SIZE]
        scores = jnp.where(allowed, matmul_nt(query, key) * scale, masked_score)
        probs = jnp.exp(scores - lse_ref[:, head : head + 1])
        prob_grad = matmul_nt(grad, value)
        delta = jnp.sum(probs * prob_grad, axis=1, keepdims=True)
        score_grad = (probs * (prob_grad - delta)).astype(BF)
        query_parts.append(matmul(score_grad, key) * scale)
        key_part = matmul_tn(score_grad, query) * scale
        value_part = matmul_tn(probs.astype(BF), grad)
        if head % sharing == 0:
            key_parts.append(key_part)
            value_parts.append(value_part)
        else:
            key_parts[-1] = key_parts[-1] + key_part
            value_parts[-1] = value_parts[-1] + value_part
    kv_out[0] = jnp.concatenate(key_parts, axis=1).astype(BF)
    key_copy.start()
    kv_out[1] = jnp.concatenate(value_parts, axis=1).astype(BF)
    value_copy.start()

    def rotate_back(array):
        wide_lanes = array.shape[1]
        lane = lax.broadcasted_iota(jnp.int32, (1, wide_lanes), 1)
        first = lane % HEAD_SIZE < HEAD_SIZE // 2
        cosines = jnp.concatenate([cos_ref[...]] * (wide_lanes // 128), axis=1)
        sines = jnp.concatenate([sin_ref[...]] * (wide_lanes // 128), axis=1)
        return (array * cosines - turn(array, first) * sines).astype(BF)

    query_grad = rotate_back(jnp.concatenate(query_parts, axis=1))
    by_rows = (parts, rows // parts, width)
    terms[pl.ds(0, parts)] = matmul_nt(query_grad, wq_ref[...]).reshape(by_rows)
    turned = n_ref[...].T
    query_part = matmul(turned, query_grad).astype(BF)
    for at in range(2):
        wide[at, :, :queries] = query_part[at * width // 2 : (at + 1) * width // 2, :]
    key_copy.wait_recv()
    value_copy.wait_recv()
    key_grad = rotate_back(kv_out[0, :rows, :].astype(F32) + kv_in[0].astype(F32))
    value_grad = (kv_out[1, :rows, :].astype(F32) + kv_in[1].astype(F32)).astype(BF)
    more = matmul_nt(key_grad, wk_ref[...]) + matmul_nt(value_grad, wv_ref[...])
    terms[pl.ds(0, parts)] += more.reshape(by_rows)
    both_part = matmul(turned, jnp.concatenate([key_grad, value_grad], axis=1)).astype(BF)
    for at in range(2):
        wide[at, :, queries:] = both_part[at * width // 2 : (at + 1) * width // 2, :]
    wide_steps[0].start()

    def gain_part(at, total):
        values = x_ref[at].astype(F32)
        return total + jnp.sum(terms[at] * (values * scale_of(values)), axis=0, keepdims=True)

    first_sum = lax.fori_loop(0, parts, gain_part, jnp.zeros((1, width), F32))
    pad = jnp.zeros((rows2.shape[0] - 2, width), F32)
    rows2[...] = jnp.concatenate([first_sum, second_ref[...], pad], axis=0).astype(BF)
    rows_steps[0].start()

    def exchange(at):
        @pl.when(at == 0)
        def _():
            rows_steps[0].wait()
            add(rows2, rows_core)
            rows_steps[1].start()

        @pl.when(at == 1)
        def _():
            wide_steps[0].wait()
            add(wide.at[core], wide_core)

        @pl.when(at == 2)
        def _():
            rows_steps[1].wait()
            add(rows2, rows_y)
            rows_steps[2].start()
            wide_steps[1].start()

        @pl.when(at == 5)
        def _():
            rows_steps[2].wait()
            add(rows2, rows_x)
            summed = rows2[...].astype(F32)
            terms[parts] = jnp.concatenate([summed[:1, :], jnp.zeros((PART - 1, width), F32)], axis=0)
            gains_ref[1:2, :] = summed[1:2, :]

        @pl.when(at == 11)
        def _():
            wide_steps[1].wait()
            add(wide.at[core], wide_x)
            wide_steps[2].start()

        @pl.when(at == 3)
        def _():
            tall_steps[2].wait()
            add(tall.at[core], tall_x)
            tall_steps[3].start()

        @pl.when(at == 20)
        def _():
            wide_steps[2].wait()
            add(wide.at[core], wide_y)
            wide_steps[3].start()

    heads = queries // HEAD_SIZE

    def body(at, carry):
        exchange(at)
        line.step(at)

        @pl.when((at % 2 == 0) & (at // 2 + heads < spread.steps))
        def _():
            spread.step(at // 2 + heads)

        @pl.when((at % 2 == 0) & (at // 2 + heads >= spread.first_whole) & (at // 2 + heads < spread.steps))
        def _():
            block = at // 2 + heads - spread.first_whole
            block_ref[block] = (res_ref[block, :, spread.own()] + spread.total(block)).astype(BF)

        part = at - LAG * line.last

        @pl.when((part >= 0) & (part < parts))
        def _():
            grad = line.total(part)
            values = x_ref[part].astype(F32)
            scale = scale_of(values)
            unit = values * scale
            grad_ref[part] = (res_grad_ref[part] + norm_back(grad, unit, scale, gain_ref[...])).astype(BF)

        return carry

    lax.fori_loop(0, parts + 1 + LAG * line.last, body, 0)
    gains_ref[0:1, :] = line.total(parts)[:1, :]
    line.drain()
    spread.drain()
    key_copy.wait_send()
    value_copy.wait_send()
    tall_steps[3].wait()
    wide_steps[3].wait()
    tall_out[...] = tall[core]
    wide_out[...] = wide[core]


class Spread:
    def __init__(self, term, from_left, from_right, to_right, to_left, sems):
        self.place = lax.axis_index("tensor")
        self.size = lax.axis_size("tensor")
        self.term = term
        self.blocks = term.shape[0]
        self.span = term.shape[2] // self.size
        self.from_left, self.from_right = from_left, from_right
        self.to_right, self.to_left = to_right, to_left
        self.sems = sems
        self.first_whole = 2 * (self.size - 1)
        self.steps = self.blocks + self.first_whole

    def copy(self, way, block, shard):
        last = self.size - 1
        near = jnp.where(self.place < last, self.place + 1, self.place - 1)
        far = jnp.where(self.place > 0, self.place - 1, self.place + 1)
        source, target, device = (
            (self.to_right, self.from_left, near) if way == 0 else (self.to_left, self.from_right, far)
        )
        return pltpu.make_async_remote_copy(
            src_ref=source.at[block, shard], dst_ref=target.at[block, shard],
            send_sem=self.sems.at[2 * way, block, shard], recv_sem=self.sems.at[2 * way + 1, block, shard],
            device_id={"tensor": device}, device_id_type=MESH,
        )

    def clear(self):
        @pl.when(self.place == 0)
        def _():
            self.from_left[...] = jnp.zeros(self.from_left.shape, BF)

        @pl.when(self.place == self.size - 1)
        def _():
            self.from_right[...] = jnp.zeros(self.from_right.shape, BF)

    def passes(self, way, shard):
        return self.place < shard if way == 0 else self.place > shard

    def has_source(self, way):
        return self.place > 0 if way == 0 else self.place < self.size - 1

    def step(self, at):
        for way in range(2):
            block = at - 2 * (self.place if way == 0 else self.size - 1 - self.place)
            valid = (block >= 0) & (block < self.blocks)
            arrived = self.from_left if way == 0 else self.from_right
            leaving = self.to_right if way == 0 else self.to_left
            for shard in range(self.size):
                here = valid & self.passes(way, shard)

                @pl.when(here & self.has_source(way))
                def _():
                    self.copy(way, block, shard).wait_recv()

                @pl.when(here)
                def _():
                    lanes = slice(shard * self.span, (shard + 1) * self.span)
                    own = self.term[block, :, lanes].astype(F32)
                    leaving[block, shard] = (own + arrived[block, shard].astype(F32)).astype(BF)
                    self.copy(way, block, shard).start()

    def own(self):
        return pl.ds(pl.multiple_of(self.place * self.span, self.span), self.span)

    def total(self, block):
        for way in range(2):

            @pl.when(self.has_source(way))
            def _():
                self.copy(way, block, self.place).wait_recv()

        sides = self.from_left[block, self.place].astype(F32) + self.from_right[block, self.place].astype(F32)
        return self.term[block, :, self.own()].astype(F32) + sides

    def drain(self):
        for way in range(2):
            for shard in range(self.size):

                @pl.when(self.passes(way, shard))
                def _():
                    for block in range(self.blocks):
                        self.copy(way, block, shard).wait_send()


BLOCK_ROWS = 128


def input_gradient(
    offsets, block_input, residual_grad, gain, normed, w_query, key_weight, value_weight, w_output, cosines, sines,
    query, keys, values, lse, attended, low, route, second, mixed, residual,
):
    rows, width = block_input.shape
    parts = rows // PART
    kv = key_weight.shape[1]
    columns = w_query.shape[1] + 2 * kv
    tall = (w_output.shape[0] + route.shape[0]) // 2
    size = lax.axis_size("tensor")
    blocks = rows // BLOCK_ROWS
    wide_half = pltpu.VMEM((width // 2, columns), BF)
    tall_half = pltpu.VMEM((tall, width), BF)
    tile = pltpu.VMEM((16, width), BF)
    mix_half = pltpu.VMEM((blocks, size, BLOCK_ROWS, width // size), BF)
    return pl.pallas_call(
        input_grad_kernel,
        out_shape=(
            jax.ShapeDtypeStruct((parts, PART, width), BF),
            jax.ShapeDtypeStruct((width // 2, columns), BF),
            jax.ShapeDtypeStruct((width // 2, columns), BF),
            jax.ShapeDtypeStruct((tall, width), BF),
            jax.ShapeDtypeStruct((tall, width), BF),
            jax.ShapeDtypeStruct((8, width), F32),
            jax.ShapeDtypeStruct((blocks, BLOCK_ROWS, width // size), BF),
        ),
        in_specs=[smem_spec()] + [vmem_spec()] * 20,
        out_specs=(vmem_spec(),) * 7,
        scratch_shapes=line_scratch(parts + 1, width)
        + [
            pltpu.VMEM((parts + 1, PART, width), F32),
            pltpu.VMEM((2, 2 * rows, kv), BF),
            pltpu.VMEM((2, rows, kv), BF),
            pltpu.SemaphoreType.DMA((2, 2)),
            pltpu.VMEM((2, width // 2, columns), BF), wide_half, wide_half, wide_half,
            pltpu.VMEM((2, tall, width), BF), tall_half, tall_half, tall_half,
            tile, tile, tile, tile,
            pltpu.SemaphoreType.DMA((2, 11)),
            mix_half, mix_half, mix_half, mix_half,
            pltpu.SemaphoreType.DMA((4, blocks, size)),
        ],
        compiler_params=pltpu.CompilerParams(
            collective_id=2, has_side_effects=True, vmem_limit_bytes=60 * MIB
        ),
        cost_estimate=LINK_COST,
        name="input_grad",
    )(
        offsets, block_input.reshape(parts, PART, width), residual_grad, gain[None], normed,
        w_query, key_weight, value_weight, w_output, cosines, sines, query, keys, values, lse, attended, low,
        route, second, mixed.reshape(blocks, BLOCK_ROWS, width), residual.reshape(blocks, BLOCK_ROWS, width),
    )


CHUNK = 512
GROUP = 4


def route_gates(token, marks, w_router):
    experts_all = w_router.shape[0]
    chosen = marks[:, :experts_all].astype(F32)
    kept = marks[:, experts_all:].astype(F32)
    logits = jnp.where(chosen > 0.0, matmul_nt(token, w_router), masked_score)
    raised = jnp.exp(logits - jnp.max(logits, axis=1, keepdims=True)) * chosen
    gate = raised / jnp.sum(raised, axis=1, keepdims=True)
    return gate, gate * kept


def hidden_terms(token, pulled, weight, gate_weights, up_weights):
    gate_in = matmul(token, gate_weights)
    up_in = matmul(token, up_weights)
    sig = 0.5 * jnp.tanh(0.5 * gate_in) + 0.5
    silu = gate_in * sig
    hidden = silu * up_in
    gated = (hidden * weight).astype(BF)
    scaled = pulled * weight
    up_grad = (scaled * silu).astype(BF)
    gate_grad = (scaled * up_in * (sig + silu * (1.0 - sig))).astype(BF)
    return hidden, gated, gate_grad, up_grad


def spread_gates(kept, column, group, hid):
    lane = lax.broadcasted_iota(jnp.int32, (1, kept.shape[1]), 1)
    weights = []
    for expert in range(group):
        gate = jnp.sum(jnp.where(lane == column + expert, kept, 0.0), axis=1, keepdims=True)
        weights.append(jnp.broadcast_to(gate, (kept.shape[0], hid)))
    return jnp.concatenate(weights, axis=1)


def expert_kernel(
    n_ref, marks_ref, wr_ref, n_hbm, own_up, peer_up, far_g0, far_m, wg_ref, wu_ref, wd_ref,
    dwg_ref, dwu_ref, dwd_ref, mix_ref, back_ref, route_ref, far_n, far_on, far_g1, far_og0, far_og1, far_om,
    gates, kept_gates, gate_grads, mix, back, nt, wgs, wus, ght, dgs, dus,
    out_g, out_u, out_d, in_g, in_u, in_d, sems, far_sems, g_ref, up_sems,
):
    step = pl.program_id(0)
    steps = pl.num_programs(0) // 2
    side = lax.axis_index("expert")
    dp = lax.axis_index("dp")
    core = lax.rem(dp, 2)
    other = other_core()
    tokens, width = n_ref.shape
    experts_all = wr_ref.shape[0]
    group, _, hid = wg_ref.shape
    chunks = tokens // CHUNK
    lane = lax.broadcasted_iota(jnp.int32, (1, experts_all), 1)

    def copies(slot):
        return [
            pltpu.make_async_remote_copy(
                src_ref=source.at[slot], dst_ref=target.at[slot],
                send_sem=sems.at[0, kind, slot], recv_sem=sems.at[1, kind, slot],
                device_id=other, device_id_type=MESH,
            )
            for kind, (source, target) in enumerate(((out_g, in_g), (out_u, in_u), (out_d, in_d)))
        ]

    half = tokens // 2
    cross = [
        plain_copy(n_hbm.at[pl.ds(at * half, half), :], far_n.at[pl.ds(at * half, half), :], far_sems, at, beside())
        for at in range(2)
    ]
    share = [
        plain_copy(far_n.at[pl.ds(at * half, half), :], far_on.at[pl.ds(at * half, half), :], far_sems, 2 + at, other)
        for at in range(2)
    ]
    peer = {"expert": 1 - side}
    turn_up = plain_copy(far_g0, far_g1, far_sems, 4, peer)
    share_up = plain_copy(far_g1, far_og1, far_sems, 5, other)
    early = [
        plain_copy(source, target, far_sems, 6 + at, other)
        for at, (source, target) in enumerate(((far_g0, far_og0), (far_m, far_om)))
    ]
    loads = [
        pltpu.make_async_copy(source, g_ref.at[pl.ds(at * half, half), :], up_sems.at[at])
        for at, source in enumerate((own_up, peer_up))
    ]

    @pl.when(step == 0)
    def _():
        for copy in loads:
            copy.start()
        meet([(True, other), (True, beside()), (True, peer)])
        for copy in cross + early + [turn_up]:
            copy.start()

        def start(at, carry):
            rows = pl.ds(pl.multiple_of(at * CHUNK, CHUNK), CHUNK)
            gate, kept_gate = route_gates(n_ref[rows, :], marks_ref[rows, :], wr_ref[...])
            gates[rows, :] = gate
            kept_gates[rows, :] = kept_gate
            mix[rows, :] = jnp.zeros((CHUNK, width), F32)
            back[rows, :] = jnp.zeros((CHUNK, width), F32)
            gate_grads[rows, :] = jnp.zeros((CHUNK, experts_all), F32)
            return carry

        lax.fori_loop(0, chunks, start, 0)
        for at in range(chunks):
            nt[:, at * CHUNK : (at + 1) * CHUNK] = n_ref[at * CHUNK : (at + 1) * CHUNK, :].T
        for copy in loads:
            copy.wait()

    @pl.when(step == steps)
    def _():
        cross[0].wait_recv()
        share[0].start()
        turn_up.wait_recv()
        share_up.start()

    for expert in range(group):
        wgs[:, expert * hid : (expert + 1) * hid] = wg_ref[expert]
        wus[:, expert * hid : (expert + 1) * hid] = wu_ref[expert]
    first = step < steps
    block = jnp.where(first, (1 - core) * steps + step, core * steps + step - steps)
    column = side * (experts_all // 2) + block * group

    for at in range(chunks):
        rows = slice(at * CHUNK, (at + 1) * CHUNK)
        token = n_ref[rows, :]
        down = wd_ref[...].reshape(group * hid, width)
        pulled = matmul_nt(g_ref[rows, :], down)
        weight = spread_gates(kept_gates[rows, :], column, group, hid)
        hidden, gated, gate_grad, up_grad = hidden_terms(token, pulled, weight, wgs[...], wus[...])
        products = hidden * pulled
        grads = gate_grads[rows, :]
        for expert in range(group):
            product = jnp.sum(products[:, expert * hid : (expert + 1) * hid], axis=1, keepdims=True)
            grads = grads + jnp.where(lane == column + expert, product, 0.0)
        gate_grads[rows, :] = grads
        ght[:, rows] = gated.T
        dgs[rows, :] = gate_grad
        dus[rows, :] = up_grad
        mix[rows, :] += matmul(gated, down)
        back[rows, :] += matmul_nt(gate_grad, wgs[...]) + matmul_nt(up_grad, wus[...])

    def weight_grads(store_rows, store_down):
        for at in range(width // CHUNK):
            rows = slice(at * CHUNK, (at + 1) * CHUNK)
            turned = nt[rows, :]
            gate_part = matmul(turned, dgs[...])
            up_part = matmul(turned, dus[...])
            for expert in range(group):
                inner = slice(expert * hid, (expert + 1) * hid)
                store_rows(expert, rows, gate_part[:, inner], up_part[:, inner])
        down_part = matmul(ght[...], g_ref[...])
        for expert in range(group):
            store_down(expert, down_part[expert * hid : (expert + 1) * hid, :])

    @pl.when(first)
    def _():
        def store_rows(expert, rows, gate_part, up_part):
            out_g[step, expert, rows, :] = gate_part.astype(BF)
            out_u[step, expert, rows, :] = up_part.astype(BF)

        def store_down(expert, part):
            out_d[step, expert] = part.astype(BF)

        weight_grads(store_rows, store_down)
        for copy in copies(step):
            copy.start()

    @pl.when(step >= steps)
    def _():
        slot = step - steps
        for copy in copies(slot):
            copy.wait_recv()

        def store_rows(expert, rows, gate_part, up_part):
            dwg_ref[expert, rows, :] = (gate_part + in_g[slot, expert, rows, :].astype(F32)).astype(BF)
            dwu_ref[expert, rows, :] = (up_part + in_u[slot, expert, rows, :].astype(F32)).astype(BF)

        def store_down(expert, part):
            dwd_ref[expert] = (part + in_d[slot, expert].astype(F32)).astype(BF)

        weight_grads(store_rows, store_down)
        for copy in copies(slot):
            copy.wait_send()

    @pl.when(step == 2 * steps - 1)
    def _():
        cross[1].wait_recv()
        share[1].start()
        route_ref[...] = jnp.zeros(route_ref.shape, F32)

        def finish(at, carry):
            rows = pl.ds(pl.multiple_of(at * CHUNK, CHUNK), CHUNK)
            mix_ref[rows, :] = mix[rows, :].astype(BF)
            grads = gate_grads[rows, :] * kept_gates[rows, :]
            chosen_grad = grads - gates[rows, :] * jnp.sum(grads, axis=1, keepdims=True)
            low = chosen_grad.astype(BF)
            back_ref[rows, :] = (back[rows, :] + matmul(low, wr_ref[...])).astype(BF)
            route_ref[...] += matmul_tn(low, n_ref[rows, :])
            return carry

        lax.fori_loop(0, chunks, finish, 0)
        for copy in cross + [turn_up]:
            copy.wait_send()
        for copy in share + early + [share_up]:
            copy.wait()


def experts(normed, marks, w_router, upstream, peer_up, far_up, far_marks, w_gate, w_up, w_down):
    tokens, width = normed.shape
    count, _, hid = w_gate.shape
    half = count // 2
    steps = half // GROUP
    experts_all = w_router.shape[0]
    once = pl.Buffered(1)
    whole = lambda step: (0, 0)

    def picked(step):
        core = lax.rem(lax.axis_index("dp"), 2)
        return (jnp.where(step < steps, (1 - core) * steps + step, core * steps + step - steps), 0, 0)

    own = lambda step: (jnp.maximum(step - steps, 0), 0, 0)
    args = [normed, marks, w_router]
    specs = [pl.BlockSpec(array.shape, whole, pipeline_mode=once) for array in args]
    args += [normed, upstream, peer_up, far_up, far_marks]
    specs += [pl.BlockSpec(memory_space=pl.ANY)] * 5
    up_block, down_block = (GROUP, width, hid), (GROUP, hid, width)
    specs += [pl.BlockSpec(up_block, picked), pl.BlockSpec(up_block, picked), pl.BlockSpec(down_block, picked)]
    gate_scratch = pltpu.VMEM((tokens, experts_all), F32)
    rows_scratch = pltpu.VMEM((tokens, width), F32)
    swap_scratch = [
        pltpu.VMEM((steps,) + up_block, BF),
        pltpu.VMEM((steps,) + up_block, BF),
        pltpu.VMEM((steps,) + down_block, BF),
    ]
    return pl.pallas_call(
        expert_kernel,
        out_shape=[
            jax.ShapeDtypeStruct((half, width, hid), BF),
            jax.ShapeDtypeStruct((half, width, hid), BF),
            jax.ShapeDtypeStruct((half, hid, width), BF),
            jax.ShapeDtypeStruct((tokens, width), BF),
            jax.ShapeDtypeStruct((tokens, width), BF),
            jax.ShapeDtypeStruct((experts_all, width), F32),
            jax.ShapeDtypeStruct((tokens, width), BF),
            jax.ShapeDtypeStruct((tokens, width), BF),
            jax.ShapeDtypeStruct(far_up.shape, BF),
            jax.ShapeDtypeStruct(far_up.shape, BF),
            jax.ShapeDtypeStruct(far_up.shape, BF),
            jax.ShapeDtypeStruct(far_marks.shape, BF),
        ],
        grid=(2 * steps,),
        in_specs=specs,
        out_specs=[
            pl.BlockSpec(up_block, own),
            pl.BlockSpec(up_block, own),
            pl.BlockSpec(down_block, own),
            pl.BlockSpec((tokens, width), whole, pipeline_mode=once),
            pl.BlockSpec((tokens, width), whole, pipeline_mode=once),
            pl.BlockSpec((experts_all, width), whole, pipeline_mode=once),
        ]
        + [pl.BlockSpec(memory_space=pl.ANY)] * 6,
        scratch_shapes=[
            gate_scratch, gate_scratch, gate_scratch, rows_scratch, rows_scratch,
            pltpu.VMEM((width, tokens), BF),
            pltpu.VMEM((width, GROUP * hid), BF),
            pltpu.VMEM((width, GROUP * hid), BF),
            pltpu.VMEM((GROUP * hid, tokens), BF),
            pltpu.VMEM((tokens, GROUP * hid), BF),
            pltpu.VMEM((tokens, GROUP * hid), BF),
        ]
        + swap_scratch
        + swap_scratch
        + [pltpu.SemaphoreType.DMA((2, 3, steps)), pltpu.SemaphoreType.DMA((2, 8)), pltpu.VMEM((tokens, width), BF), pltpu.SemaphoreType.DMA((2,))],
        compiler_params=pltpu.CompilerParams(
            dimension_semantics=("arbitrary",), collective_id=3, has_side_effects=True, vmem_limit_bytes=60 * MIB
        ),
        cost_estimate=pl.CostEstimate(
            flops=18 * tokens * width * count * hid,
            bytes_accessed=12 * count * width * hid,
            transcendentals=tokens * count * hid,
        ),
        name="experts",
    )(*args, w_gate, w_up, w_down)


def finish_kernel(core_ref, *refs):
    ins, outs = refs[:13], refs[13:]
    part, at = pl.program_id(0), pl.program_id(1)
    mine, other = ins[:3], ins[3:6]
    wide_mine, wide_other, tall_mine, tall_other, gains, grad, block = ins[6:]
    out_g, out_u, out_d, out_q, out_k, out_v, out_o, out_r, out_first, out_second, out_grad, out_block = outs
    for place, sources in enumerate((mine, other)):

        @pl.when(part == place)
        def _():
            for source, target in zip(sources, (out_g, out_u, out_d)):
                target[...] = source[...].astype(F32)

    core = core_ref[0]
    queries, kv = out_q.shape[1], out_k.shape[1]
    half = out_q.shape[0] // 2
    tall = tall_mine.shape[0]
    outs_rows = out_o.shape[0]

    @pl.when((part == 0) & (at == 0))
    def _():
        out_grad[...] = grad[...]
        out_block[...] = block[...]
        out_first[...] = gains[0:1, :]
        out_second[...] = gains[1:2, :]

    for place in range(2):

        @pl.when((part == 0) & (at == 1 + place))
        def _():
            own = core == place
            summed = jnp.where(own, wide_mine[...].astype(F32), wide_other[...].astype(F32))
            rows = slice(place * half, (place + 1) * half)
            out_q[rows, :] = summed[:, :queries]
            out_k[rows, :] = summed[:, queries : queries + kv]
            out_v[rows, :] = summed[:, queries + kv :]
            tall_sum = jnp.where(own, tall_mine[...].astype(F32), tall_other[...].astype(F32))
            top = min((place + 1) * tall, outs_rows)
            out_o[place * tall : top, :] = tall_sum[: top - place * tall, :]
            if place == 1:
                out_r[...] = tall_sum[top - place * tall :, :]


def finish(core, sums, others, wide, wide_back, tall, tall_back, gains, grad, block, queries, outs_rows):
    half = sums[0].shape[0]
    width = grad.shape[1]
    kv = (wide.shape[1] - queries) // 2
    experts_all = 2 * tall.shape[0] - outs_rows
    whole = lambda shape: pl.BlockSpec(shape, lambda part, at, core: (0,) * len(shape), pipeline_mode=pl.Buffered(1))
    single = lambda array, index: pl.BlockSpec((1,) + array.shape[1:], index)
    first = lambda part, at, core: (jnp.where(part == 0, at, half - 1), 0, 0)
    second = lambda part, at, core: (jnp.where(part == 0, 0, at), 0, 0)
    placed = lambda part, at, core: (jnp.where(part == 0, core[0], 1 - core[0]) * half + at, 0, 0)
    rest = [wide, wide_back, tall, tall_back, gains, grad, block]
    wide_shape = lambda shape: jax.ShapeDtypeStruct(shape, F32)
    shapes = [
        (2 * wide.shape[0], queries), (2 * wide.shape[0], kv), (2 * wide.shape[0], kv),
        (outs_rows, width), (experts_all, width), (1, width), (1, width),
    ]
    return pl.pallas_call(
        finish_kernel,
        out_shape=[wide_shape((2 * half,) + item.shape[1:]) for item in sums]
        + [wide_shape(shape) for shape in shapes]
        + [jax.ShapeDtypeStruct(grad.shape, BF), jax.ShapeDtypeStruct(block.shape, BF)],
        grid_spec=pltpu.PrefetchScalarGridSpec(
            num_scalar_prefetch=1,
            grid=(2, half),
            in_specs=[single(item, first) for item in sums]
            + [single(item, second) for item in others]
            + [whole(item.shape) for item in rest],
            out_specs=[single(item, placed) for item in sums]
            + [whole(shape) for shape in shapes + [grad.shape, block.shape]],
        ),
        compiler_params=pltpu.CompilerParams(vmem_limit_bytes=60 * MIB),
        name="finish",
    )(core, *sums, *others, *rest)


def fast_device(
    block_input, first_gain, w_query, key_weight, value_weight, w_output, second_gain, w_router,
    w_gate, w_up, w_down, expert_ids, slot_index, piece_start_offsets, upstream,
):
    rows, width = block_input.shape
    experts_all = w_router.shape[1]
    core = lax.axis_index("dp") % 2
    positions = lax.axis_index("expert") * rows + jnp.arange(rows, dtype=jnp.int32)
    lanes = jnp.arange(128, dtype=jnp.int32) % (HEAD_SIZE // 2)
    inverse = jnp.exp(lanes.astype(F32) * (-2.0 * math.log(rope_base) / HEAD_SIZE))
    angle = positions.astype(F32)[:, None] * inverse[None, :]
    cosines, sines = jnp.cos(angle), jnp.sin(angle)
    routes = w_router.T
    (
        first_normed, query_rot, keys, values, attended, lse, residual, normed_all, marks, far_marks, peer_up, far_up,
    ) = front(
        piece_start_offsets, block_input, first_gain, second_gain, w_query, key_weight, value_weight, w_output,
        cosines, sines, expert_ids.T, slot_index.T, upstream, experts_all,
    )
    keys, values = keys.reshape(2 * rows, -1), values.reshape(2 * rows, -1)
    normed_all = normed_all.reshape(2 * rows, width)
    marks = marks.reshape(2 * rows, 2 * experts_all)
    far_marks = far_marks.reshape(2 * rows, 2 * experts_all)
    dwg, dwu, dwd, mix, back, route, *far = experts(
        normed_all, marks, routes, upstream, peer_up, far_up, far_marks, w_gate, w_up, w_down
    )
    far_normed, far_other_normed, far_peer_up, far_other_up, far_other_peer_up, far_other_marks = far
    residual_grad, residual_low, grad_second, route, mixed, sums = residual_gradient(
        back, mix, route, residual, upstream, second_gain, routes,
        (
            far_normed, far_other_normed, far_up, far_peer_up, far_other_up, far_other_peer_up,
            far_marks, far_other_marks,
        ),
        w_gate, w_up, w_down, (dwg, dwu, dwd),
    )
    grad_input, wide, wide_back, tall, tall_back, gains, block_output = input_gradient(
        piece_start_offsets, block_input, residual_grad, first_gain, first_normed, w_query, key_weight, value_weight,
        w_output, cosines, sines, query_rot, keys, values, lse, attended, residual_low, route, grad_second, mixed, residual,
    )
    grad_gate, grad_up, grad_down, grad_query, grad_key, grad_value, grad_output, grad_router, first, second, grad, block = finish(
        core[None].astype(jnp.int32), sums[:3], sums[3:], wide, wide_back, tall, tall_back, gains,
        grad_input.reshape(rows, width), block_output.reshape(rows, width // 4), w_query.shape[1], w_output.shape[0],
    )
    return (
        block, grad, first[0], grad_query, grad_key, grad_value, grad_output, second[0], grad_router.T,
        grad_gate, grad_up, grad_down,
    )


def solution(mesh):
    fast = mesh.shape["expert"] == 2 and mesh.shape["dp"] == 4 and mesh.shape["tensor"] == 4
    placed = (
        P(("dp", "expert"), None),
        P(),
        P(None, "tensor"),
        P(None, "tensor"),
        P(None, "tensor"),
        P("tensor", None),
        P(),
        P(),
        P("expert", None, "tensor"),
        P("expert", None, "tensor"),
        P("expert", "tensor", None),
        P(("dp", "expert"), None),
        P(("dp", "expert"), None),
        P("dp", None),
        P(("dp", "expert"), None),
    )
    return jax.shard_map(
        fast_device if fast else general_device,
        mesh=mesh,
        in_specs=placed,
        out_specs=(
            P(("dp", "expert"), "tensor"),
            P(("dp", "expert"), None),
            P(),
            P(None, "tensor"),
            P(None, "tensor"),
            P(None, "tensor"),
            P("tensor", None),
            P(),
            P(),
            P("expert", None, "tensor"),
            P("expert", None, "tensor"),
            P("expert", "tensor", None),
        ),
        check_vma=False,
    )
```

profile of v0, /device:TPU:0, one launch (start us, length us, event | category | flops | bytes accessed | tf_op | source)
XLA Modules:
  0.0 278.5 jit_solution(11836164450041548135)
XLA Ops:
  0.7 1.8 multiply_sine_fusion
  2.5 64.2 %front.1 = (bf16[512,1024]{1,0:T(8,128)(2,1)}, bf16[512,256]{1,0:T(8,128)(2,1)}, bf16[2,512,128]{2,1,0:T(8,128)(2,1)}, bf16[2,512,128]{2,1,0:T(8,128)(2,1)}, bf1...) custom-call(s32[1,2]{1,0:T(1,128)} %offsets_ref.3, ...), custom_call_target="tpu_custom_call" | custom-call | flops 40000000000 | bytes 10000000 | tf_op jit(solution)/shard_map/front/pallas_call | solution.py:728
  66.7 59.4 %experts.1 = (bf16[8,1024,128]{2,1,0:T(8,128)(2,1)}, bf16[8,1024,128]{2,1,0:T(8,128)(2,1)}, bf16[8,128,1024]{2,1,0:T(8,128)(2,1)}, bf16[1024,1024]{1,0:T(8,128)(...) custom-call(bf16[1024,1024]{1,0:T(8,128)(2,1)} %bitcast.42, ...), custom_call_target="tpu_custom_call" | custom-call | flops 38654705664 | bytes 25165824 | tf_op jit(solution)/shard_map/experts/pallas_call | solution.py:1645
  126.1 61.6 %residual_grad.1 = (f32[16,32,1024]{2,1,0:T(8,128)}, bf16[16,32,1024]{2,1,0:T(8,128)(2,1)}, f32[1,1024]{1,0:T(1,128)}, f32[32,1024]{1,0:T(8,128)}, bf16[16,32,10...) custom-call(bf16[2,16,32,1024]{3,2,1,0:T(8,128)(2,1)} %bitcast.41, ...), custom_call_target="tpu_custom_call" | custom-call | flops 40000000000 | bytes 10000000 | tf_op jit(solution)/shard_map/residual_grad/pallas_call | solution.py:1002
  187.8 70.2 %input_grad.1 = (bf16[16,32,1024]{2,1,0:T(8,128)(2,1)}, bf16[512,512]{1,0:T(8,128)(2,1)}, bf16[512,512]{1,0:T(8,128)(2,1)}, bf16[144,1024]{1,0:T(8,128)(2,1)}, b...) custom-call(s32[1,2]{1,0:T(1,128)} %offsets_ref.3, bf16[16,32,1024]{2,1,0:T(8,128)(2,1)} %bitcast.27, ...), custom_call_target="tpu_custom_call" | custom-call | flops 40000000000 | bytes 10000000 | tf_op jit(solution)/shard_map/input_grad/pallas_call | solution.py:1372
  258.0 20.1 %finish.1 = (f32[16,1024,128]{2,1,0:T(8,128)}, f32[16,1024,128]{2,1,0:T(8,128)}, f32[16,128,1024]{2,1,0:T(8,128)}, f32[1024,256]{1,0:T(8,128)}, f32[1024,128]{1,...) custom-call(s32[1]{0:T(128)} %bitcast.core_ref, ...), custom_call_target="tpu_custom_call" | custom-call | tf_op jit(solution)/shard_map/finish/pallas_call | solution.py:1755
  (2 shorter events, 0.0 us)
where the time goes:
time: 284 us; the launch traced here: 279 us
  Pallas kernels  276 us (97%)
    pallas_call x1, Pallas kernels, input_gradient(): pl.pallas_call(input_grad_kernel, out_shape=(jax.ShapeDtypeStruct((parts,...  70.2 us
    pallas_call x1, Pallas kernels, front(): pl.pallas_call(front_kernel, out_shape=(low(rows, width), low(rows, queri...  64.2 us
    pallas_call x1, Pallas kernels, residual_gradient(): pl.pallas_call(residual_grad_kernel, out_shape=[jax.ShapeDtypeStruct((par...  61.6 us
    pallas_call x1, Pallas kernels, experts(): pl.pallas_call(expert_kernel, out_shape=[jax.ShapeDtypeStruct((half, widt...  59.4 us
    pallas_call x1, Pallas kernels, finish(): pl.pallas_call(finish_kernel, out_shape=[wide_shape((2 * half,) + item.sh...  20.1 us

commit v1 on v0

--- a/solution.py
+++ b/solution.py
@@ -494,7 +494,8 @@
 
 
 class Line:
-    def __init__(self, parts, term, from_left, from_right, to_right, to_left, sems):
+    def __init__(self, parts, term, from_left, from_right, to_right, to_left, sems, lag=LAG):
+        self.lag = lag
         self.place = lax.axis_index("tensor")
         self.last = lax.axis_size("tensor") - 1
         self.parts = parts
@@ -529,7 +530,7 @@
 
     def step(self, at):
         for way in range(2):
-            part = at - LAG * (self.place if way == 0 else self.last - self.place)
+            part = at - self.lag * (self.place if way == 0 else self.last - self.place)
             has_source = self.place > 0 if way == 0 else self.place < self.last
             has_target = self.place < self.last if way == 0 else self.place > 0
             arrived = self.from_left if way == 0 else self.from_right
@@ -563,8 +564,8 @@
         lax.fori_loop(0, self.parts, wait, 0)
 
 
-def line_scratch(parts, width):
-    return [pltpu.VMEM((parts, PART, width), BF)] * 4 + [pltpu.SemaphoreType.DMA((4, parts))]
+def line_scratch(parts, width, part=PART):
+    return [pltpu.VMEM((parts, part, width), BF)] * 4 + [pltpu.SemaphoreType.DMA((4, parts))]
 
 
 def peer_copy(source, target, sems, at):
@@ -761,35 +762,46 @@
 
 
 UNIT = 512
+BIG_PART = 64
+BIG_LAG = 2
 SUB = 256
 
 
 def residual_grad_kernel(
-    back_ref, route_ref, res_ref, up_ref, gain_ref, wr_ref, mix_ref,
+    route_ref, gain_ref, wr_ref, back_hbm, mix_hbm, res_hbm, up_hbm,
     far_n, far_on, far_g0, far_g1, far_og0, far_og1, far_m, far_om,
     wg_hbm, wu_hbm, wd_hbm, pg_hbm, pu_hbm, pd_hbm,
     grad_ref, low_ref, second_ref, route_out, mixed_ref, sg_hbm, su_hbm, sd_hbm, og_hbm, ou_hbm, od_hbm,
     from_left, from_right, to_right, to_left, sems, peer_sems, arrived, terms,
     tokens_n, tokens_g, turned, kept_gates, gates_w, ups_w, downs_w, pair_g, pair_u, pair_d, ght, dgs, dus,
     row_sems, weight_sems, pair_sems, out_sems, mix_arrived, mix_sems, marks_ref, share_sems,
+    back_ref, mix_ref, res_ref, up_ref, load_sems,
 ):
-    parts = back_ref.shape[1]
+    parts = back_ref.shape[0]
     core = lax.rem(lax.axis_index("dp"), 2)
     side = lax.axis_index("expert")
     groups, group, width, hid = pair_g.shape
     experts_all = wr_ref.shape[0]
-    line = Line(parts + 1, lambda at: terms[at], from_left, from_right, to_right, to_left, sems)
+    line = Line(parts + 1, lambda at: terms[at], from_left, from_right, to_right, to_left, sems, BIG_LAG)
+    loads = [
+        pltpu.make_async_copy(source, target, load_sems.at[at])
+        for at, (source, target) in enumerate(
+            ((back_hbm.at[0], back_ref), (res_hbm, res_ref), (up_hbm, up_ref), (mix_hbm.at[0], mix_ref))
+        )
+    ]
+    for copy in loads:
+        copy.start()
     line.clear()
     meet(line_partners() + [(True, {"expert": 1 - side}), (True, other_core())])
 
     def send(part, carry):
-        peer_copy(back_ref.at[1, part], arrived.at[part], peer_sems, part).start()
+        peer_copy(back_hbm.at[1, part], arrived.at[part], peer_sems, part).start()
         return carry
 
     lax.fori_loop(0, parts, send, 0)
 
     def send_mix(part, carry):
-        peer_copy(mix_ref.at[1, part], mix_arrived.at[part], mix_sems, part).start()
+        peer_copy(mix_hbm.at[1, part], mix_arrived.at[part], mix_sems, part).start()
         return carry
 
     lax.fori_loop(0, parts, send_mix, 0)
@@ -843,7 +855,9 @@
         )
     for copy in row_copies[:4] + weight_copies[0] + row_copies[4:] + pair_copies[0] + weight_copies[1] + pair_copies[1]:
         copy.start()
-    terms[parts] = route_ref[...]
+    pad = jnp.zeros((BIG_PART - route_ref.shape[0], route_ref.shape[1]), F32)
+    terms[parts] = jnp.concatenate([route_ref[...], pad], axis=0)
+    loads[0].wait()
     second_ref[...] = jnp.zeros(second_ref.shape, F32)
     chunks = 2 * half // UNIT
     units = chunks + 3
@@ -925,19 +939,19 @@
                     copy.start()
 
     def add_mix(part):
-        peer_copy(mix_ref.at[1, part], mix_arrived.at[part], mix_sems, part).wait_recv()
-        mixed_ref[part] = (mix_ref[0, part].astype(F32) + mix_arrived[part].astype(F32)).astype(BF)
-
-    steps = parts + 1 + LAG * line.last
+        peer_copy(mix_hbm.at[1, part], mix_arrived.at[part], mix_sems, part).wait_recv()
+        mixed_ref[part] = (mix_ref[part].astype(F32) + mix_arrived[part].astype(F32)).astype(BF)
+
+    steps = parts + 1 + BIG_LAG * line.last
 
     def advance(at):
         @pl.when(at < parts)
         def _():
-            peer_copy(back_ref.at[1, at], arrived.at[at], peer_sems, at).wait_recv()
-            terms[at] = back_ref[0, at].astype(F32) + arrived[at].astype(F32)
+            peer_copy(back_hbm.at[1, at], arrived.at[at], peer_sems, at).wait_recv()
+            terms[at] = back_ref[at].astype(F32) + arrived[at].astype(F32)
 
         line.step(at)
-        part = at - LAG * line.last
+        part = at - BIG_LAG * line.last
 
         @pl.when((part >= 0) & (part < parts))
         def _():
@@ -954,33 +968,34 @@
         def _():
             add_mix(at - MIX_STEP)
 
-    turns = max(groups * units, (steps + 1) // 2)
+    turns = max(groups * units, steps)
 
     def body(at, carry):
         @pl.when(at < groups * units)
         def _():
             compute(at)
 
-        def pair(half, carry):
-            advance(2 * at + half)
-            return carry
-
-        lax.fori_loop(0, 2, pair, 0)
+        @pl.when(at == 2)
+        def _():
+            for copy in loads[1:]:
+                copy.wait()
+
+        advance(at)
         return carry
 
     lax.fori_loop(0, turns, body, 0)
-    route_out[...] = line.total(parts)
+    route_out[...] = line.total(parts)[: route_ref.shape[0], :]
 
     def rest(part, carry):
         add_mix(part)
         return carry
 
-    lax.fori_loop(2 * turns - MIX_STEP, parts, rest, 0)
+    lax.fori_loop(turns - MIX_STEP, parts, rest, 0)
     line.drain()
 
     def wait(part, carry):
-        peer_copy(back_ref.at[1, part], arrived.at[part], peer_sems, part).wait_send()
-        peer_copy(mix_ref.at[1, part], mix_arrived.at[part], mix_sems, part).wait_send()
+        peer_copy(back_hbm.at[1, part], arrived.at[part], peer_sems, part).wait_send()
+        peer_copy(mix_hbm.at[1, part], mix_arrived.at[part], mix_sems, part).wait_send()
         return carry
 
     lax.fori_loop(0, parts, wait, 0)
@@ -989,12 +1004,12 @@
             copy.wait()
 
 
-MIX_STEP = 17
+MIX_STEP = 9
 
 
 def residual_gradient(back, mix, route, residual, upstream, gain, w_router, far_rows, w_gate, w_up, w_down, pairs):
     rows, width = upstream.shape
-    parts = rows // PART
+    parts = rows // BIG_PART
     half, _, hid = pairs[0].shape
     groups = half // GROUP
     tokens = 2 * far_rows[0].shape[0]
@@ -1002,20 +1017,20 @@
     grad, low, second, route, mixed, *sums = pl.pallas_call(
         residual_grad_kernel,
         out_shape=[
-            jax.ShapeDtypeStruct((parts, PART, width), F32),
-            jax.ShapeDtypeStruct((parts, PART, width), BF),
+            jax.ShapeDtypeStruct((parts, BIG_PART, width), F32),
+            jax.ShapeDtypeStruct((parts, BIG_PART, width), BF),
             jax.ShapeDtypeStruct((1, width), F32),
             jax.ShapeDtypeStruct(route.shape, F32),
-            jax.ShapeDtypeStruct((parts, PART, width), BF),
+            jax.ShapeDtypeStruct((parts, BIG_PART, width), BF),
         ]
         + [jax.ShapeDtypeStruct(pair.shape, BF) for pair in pairs] * 2,
-        in_specs=[vmem_spec()] * 7 + [any_spec] * 14,
+        in_specs=[vmem_spec()] * 3 + [any_spec] * 18,
         out_specs=[vmem_spec()] * 5 + [any_spec] * 6,
-        scratch_shapes=line_scratch(parts + 1, width)
+        scratch_shapes=line_scratch(parts + 1, width, BIG_PART)
         + [
             pltpu.SemaphoreType.DMA((2, parts)),
-            pltpu.VMEM((parts, PART, width), BF),
-            pltpu.VMEM((parts + 1, PART, width), F32),
+            pltpu.VMEM((parts, BIG_PART, width), BF),
+            pltpu.VMEM((parts + 1, BIG_PART, width), F32),
             pltpu.VMEM((tokens, width), BF),
             pltpu.VMEM((tokens, width), BF),
             pltpu.VMEM((width, tokens), BF),
@@ -1033,10 +1048,15 @@
             pltpu.SemaphoreType.DMA((groups, 3, GROUP)),
             pltpu.SemaphoreType.DMA((groups, 3)),
             pltpu.SemaphoreType.DMA((groups, 3)),
-            pltpu.VMEM((parts, PART, width), BF),
+            pltpu.VMEM((parts, BIG_PART, width), BF),
             pltpu.SemaphoreType.DMA((2, parts)),
             pltpu.VMEM((tokens, 2 * w_router.shape[0]), BF),
             pltpu.SemaphoreType.DMA((groups, 2, 3)),
+            pltpu.VMEM((parts, BIG_PART, width), BF),
+            pltpu.VMEM((parts, BIG_PART, width), BF),
+            pltpu.VMEM((parts, BIG_PART, width), F32),
+            pltpu.VMEM((parts, BIG_PART, width), BF),
+            pltpu.SemaphoreType.DMA((4,)),
         ],
         compiler_params=pltpu.CompilerParams(
             collective_id=1, has_side_effects=True, vmem_limit_bytes=60 * MIB
@@ -1044,19 +1064,19 @@
         cost_estimate=LINK_COST,
         name="residual_grad",
     )(
-        back.reshape(2, parts, PART, width), route, residual, upstream.reshape(parts, PART, width), gain[None],
-        w_router, mix.reshape(2, parts, PART, width), *far_rows, w_gate, w_up, w_down, *pairs,
+        route, gain[None], w_router, back.reshape(2, parts, BIG_PART, width), mix.reshape(2, parts, BIG_PART, width),
+        residual.reshape(parts, BIG_PART, width), upstream.reshape(parts, BIG_PART, width), *far_rows, w_gate, w_up, w_down, *pairs,
     )
     return grad, low.reshape(rows, width), second, route, mixed, sums
 
 
 def input_grad_kernel(
-    offsets_ref, x_ref, res_grad_ref, gain_ref, n_ref, wq_ref, wk_ref, wv_ref, wo_ref, cos_ref, sin_ref,
-    q_ref, k_ref, v_ref, lse_ref, att_ref, low_ref, route_ref, second_ref, mix_ref, res_ref,
+    offsets_ref, gain_ref, wq_ref, wk_ref, wv_ref, wo_ref, cos_ref, sin_ref,
+    q_ref, k_ref, v_ref, lse_ref, att_ref, low_ref, route_ref, second_ref, mix_ref, x_hbm, res_grad_hbm, n_hbm, res_hbm,
     grad_ref, wide_out, wide_back, tall_out, tall_back, gains_ref, block_ref,
     from_left, from_right, to_right, to_left, sems, terms, kv_out, kv_in, kv_sems,
     wide, wide_core, wide_x, wide_y, tall, tall_core, tall_x, tall_y, rows2, rows_core, rows_x, rows_y, sum_sems,
-    mix_left, mix_right, mix_to_right, mix_to_left, mix_sems,
+    mix_left, mix_right, mix_to_right, mix_to_left, mix_sems, x_ref, res_grad_ref, n_ref, res_ref, load_sems,
 ):
     parts = x_ref.shape[0]
     rows = n_ref.shape[0]
@@ -1067,6 +1087,14 @@
     queries = wq_ref.shape[1]
     line = Line(parts + 1, lambda at: terms[at], from_left, from_right, to_right, to_left, sems)
     spread = Spread(mix_ref, mix_left, mix_right, mix_to_right, mix_to_left, mix_sems)
+    loads = [
+        pltpu.make_async_copy(source, target, load_sems.at[at])
+        for at, (source, target) in enumerate(
+            ((n_hbm, n_ref), (x_hbm, x_ref), (res_grad_hbm, res_grad_ref), (res_hbm, res_ref))
+        )
+    ]
+    for copy in loads:
+        copy.start()
     line.clear()
     spread.clear()
     meet(line_partners() + [(True, peer), (True, beside()), (True, other_core())])
@@ -1156,6 +1184,8 @@
         sines = jnp.concatenate([sin_ref[...]] * (wide_lanes // 128), axis=1)
         return (array * cosines - turn(array, first) * sines).astype(BF)
 
+    for copy in loads:
+        copy.wait()
     query_grad = rotate_back(jnp.concatenate(query_parts, axis=1))
     by_rows = (parts, rows // parts, width)
     terms[pl.ds(0, parts)] = matmul_nt(query_grad, wq_ref[...]).reshape(by_rows)
@@ -1380,7 +1410,7 @@
             jax.ShapeDtypeStruct((8, width), F32),
             jax.ShapeDtypeStruct((blocks, BLOCK_ROWS, width // size), BF),
         ),
-        in_specs=[smem_spec()] + [vmem_spec()] * 20,
+        in_specs=[smem_spec()] + [vmem_spec()] * 16 + [pl.BlockSpec(memory_space=pl.ANY)] * 4,
         out_specs=(vmem_spec(),) * 7,
         scratch_shapes=line_scratch(parts + 1, width)
         + [
@@ -1394,6 +1424,11 @@
             pltpu.SemaphoreType.DMA((2, 11)),
             mix_half, mix_half, mix_half, mix_half,
             pltpu.SemaphoreType.DMA((4, blocks, size)),
+            pltpu.VMEM((parts, PART, width), BF),
+            pltpu.VMEM((parts, PART, width), F32),
+            pltpu.VMEM((rows, width), BF),
+            pltpu.VMEM((blocks, BLOCK_ROWS, width), F32),
+            pltpu.SemaphoreType.DMA((4,)),
         ],
         compiler_params=pltpu.CompilerParams(
             collective_id=2, has_side_effects=True, vmem_limit_bytes=60 * MIB
@@ -1401,9 +1436,9 @@
         cost_estimate=LINK_COST,
         name="input_grad",
     )(
-        offsets, block_input.reshape(parts, PART, width), residual_grad, gain[None], normed,
-        w_query, key_weight, value_weight, w_output, cosines, sines, query, keys, values, lse, attended, low,
-        route, second, mixed.reshape(blocks, BLOCK_ROWS, width), residual.reshape(blocks, BLOCK_ROWS, width),
+        offsets, gain[None], w_query, key_weight, value_weight, w_output, cosines, sines, query, keys, values, lse,
+        attended, low, route, second, mixed.reshape(blocks, BLOCK_ROWS, width), block_input.reshape(parts, PART, width),
+        residual_grad.reshape(parts, PART, width), normed, residual.reshape(blocks, BLOCK_ROWS, width),
     )
 
 
@@ -1721,7 +1756,7 @@
 
     for place in range(2):
 
-        @pl.when((part == 0) & (at == 1 + place))
+        @pl.when((part == place) & (at == 1))
         def _():
             own = core == place
             summed = jnp.where(own, wide_mine[...].astype(F32), wide_other[...].astype(F32))
@@ -1742,10 +1777,12 @@
     kv = (wide.shape[1] - queries) // 2
     experts_all = 2 * tall.shape[0] - outs_rows
     whole = lambda shape: pl.BlockSpec(shape, lambda part, at, core: (0,) * len(shape), pipeline_mode=pl.Buffered(1))
-    single = lambda array, index: pl.BlockSpec((1,) + array.shape[1:], index)
-    first = lambda part, at, core: (jnp.where(part == 0, at, half - 1), 0, 0)
+    step = 4
+    count = half // step
+    single = lambda array, index: pl.BlockSpec((step,) + array.shape[1:], index)
+    first = lambda part, at, core: (jnp.where(part == 0, at, count - 1), 0, 0)
     second = lambda part, at, core: (jnp.where(part == 0, 0, at), 0, 0)
-    placed = lambda part, at, core: (jnp.where(part == 0, core[0], 1 - core[0]) * half + at, 0, 0)
+    placed = lambda part, at, core: (jnp.where(part == 0, core[0], 1 - core[0]) * count + at, 0, 0)
     rest = [wide, wide_back, tall, tall_back, gains, grad, block]
     wide_shape = lambda shape: jax.ShapeDtypeStruct(shape, F32)
     shapes = [
@@ -1759,7 +1796,7 @@
         + [jax.ShapeDtypeStruct(grad.shape, BF), jax.ShapeDtypeStruct(block.shape, BF)],
         grid_spec=pltpu.PrefetchScalarGridSpec(
             num_scalar_prefetch=1,
-            grid=(2, half),
+            grid=(2, count),
             in_specs=[single(item, first) for item in sums]
             + [single(item, second) for item in others]
             + [whole(item.shape) for item in rest],

time: 284 us -> 272 us (0.958)
  Pallas kernels: 276 us -> 265 us
    pallas_call x1, Pallas kernels: 61.6 us -> 55.9 us  [residual_gradient(): pl.pallas_call(residual_grad_kernel, out_shape=[jax.ShapeDtypeStruct((par...]
    pallas_call x1, Pallas kernels: 20.1 us -> 15.9 us  [finish(): pl.pallas_call(finish_kernel, out_shape=[wide_shape((2 * half,) + item.sh...]
where the time goes in v1:
time: 272 us; the launch traced here: 267 us
  Pallas kernels  265 us (97%)
    pallas_call x1, Pallas kernels, input_gradient(): pl.pallas_call(input_grad_kernel, out_shape=(jax.ShapeDtypeStruct((parts,...  69 us
    pallas_call x1, Pallas kernels, front(): pl.pallas_call(front_kernel, out_shape=(low(rows, width), low(rows, queri...  64.2 us
    pallas_call x1, Pallas kernels, experts(): pl.pallas_call(expert_kernel, out_shape=[jax.ShapeDtypeStruct((half, widt...  59.6 us
    pallas_call x1, Pallas kernels, residual_gradient(): pl.pallas_call(residual_grad_kernel, out_shape=[jax.ShapeDtypeStruct((par...  55.9 us
    pallas_call x1, Pallas kernels, finish(): pl.pallas_call(finish_kernel, out_shape=[wide_shape((2 * half,) + item.sh...  15.9 us

profile of v1, /device:TPU:0, one launch (start us, length us, event | category | flops | bytes accessed | tf_op | source)
XLA Modules:
  0.0 267.4 jit_solution(15368207409941579381)
XLA Ops:
  0.7 1.8 multiply_sine_fusion
  2.5 64.2 %front.1 = (bf16[512,1024]{1,0:T(8,128)(2,1)}, bf16[512,256]{1,0:T(8,128)(2,1)}, bf16[2,512,128]{2,1,0:T(8,128)(2,1)}, bf16[2,512,128]{2,1,0:T(8,128)(2,1)}, bf1...) custom-call(s32[1,2]{1,0:T(1,128)} %offsets_ref.3, ...), custom_call_target="tpu_custom_call" | custom-call | flops 40000000000 | bytes 10000000 | tf_op jit(solution)/shard_map/front/pallas_call | solution.py:729
  66.7 59.6 %experts.1 = (bf16[8,1024,128]{2,1,0:T(8,128)(2,1)}, bf16[8,1024,128]{2,1,0:T(8,128)(2,1)}, bf16[8,128,1024]{2,1,0:T(8,128)(2,1)}, bf16[1024,1024]{1,0:T(8,128)(...) custom-call(bf16[1024,1024]{1,0:T(8,128)(2,1)} %bitcast.46, ...), custom_call_target="tpu_custom_call" | custom-call | flops 38654705664 | bytes 25165824 | tf_op jit(solution)/shard_map/experts/pallas_call | solution.py:1680
  126.3 55.9 %residual_grad.1 = (f32[8,64,1024]{2,1,0:T(8,128)}, bf16[8,64,1024]{2,1,0:T(8,128)(2,1)}, f32[1,1024]{1,0:T(1,128)}, f32[32,1024]{1,0:T(8,128)}, bf16[8,64,1024]...) custom-call(f32[32,1024]{1,0:T(8,128)} %get-tuple-element.71.route_r, ...), custom_call_target="tpu_custom_call" | custom-call | flops 40000000000 | bytes 10000000 | tf_op jit(solution)/shard_map/residual_grad/pallas_call | solution.py:1017
  182.3 69.0 %input_grad.1 = (bf16[16,32,1024]{2,1,0:T(8,128)(2,1)}, bf16[512,512]{1,0:T(8,128)(2,1)}, bf16[512,512]{1,0:T(8,128)(2,1)}, bf16[144,1024]{1,0:T(8,128)(2,1)}, b...) custom-call(s32[1,2]{1,0:T(1,128)} %offsets_ref.3, f32[1,1024]{1,0:T(1,128)} %bitcast.38, ...), custom_call_target="tpu_custom_call" | custom-call | flops 40000000000 | bytes 10000000 | tf_op jit(solution)/shard_map/input_grad/pallas_call | solution.py:1402
  251.3 15.9 %finish.1 = (f32[16,1024,128]{2,1,0:T(8,128)}, f32[16,1024,128]{2,1,0:T(8,128)}, f32[16,128,1024]{2,1,0:T(8,128)}, f32[1024,256]{1,0:T(8,128)}, f32[1024,128]{1,...) custom-call(s32[1]{0:T(128)} %bitcast.core_ref, ...), custom_call_target="tpu_custom_call" | custom-call | tf_op jit(solution)/shard_map/finish/pallas_call | solution.py:1792
  (2 shorter events, 0.0 us)
